TPU v7x, 256 devices: a whole 4x4x8 slice. The times are simulated.
256 devices in a mesh: row: 16 (over z, core), col: 16 (over x, y).
Axes of the slice: x: 4, y: 4, z: 8, core: 2. Of those that a mesh axis runs over, the one named last changes fastest.
Arguments:
- hidden: bfloat16 [16, 2048, 2560], P('row', 'col'), may hold values from -6 to 6
- grad_out: bfloat16 [16, 2048, 2560], P('row', 'col'), may hold values from -6 to 6
- w_key: bfloat16 [1280, 2560], P('row'), may hold values from -0.15625 to 0.15625
- w_value: bfloat16 [1280, 2560], P('row'), may hold values from -0.15625 to 0.15625
- depthwise_weight: float32 [4, 2560], replicated, may hold values from -3 to 3
- table: float32 [10240, 1280], P(('row', 'col')), may hold values from -6 to 6
- adam_m: float32 [10240, 1280], P(('row', 'col')), may hold values from -4 to 4
- adam_v: float32 [10240, 1280], P(('row', 'col')), may hold values from 0.25 to 4
- row_owner: int32 [16, 2304, 1], P('row', 'col'), may hold values from 0 to 255; in each aligned block of 144 rows (0 to 143, 144 to 287, ..., all dimensions but the last counted through in order) at most 2 rows name the same one
- row_local: int32 [16, 2304], P('row', 'col'), may hold values from 0 to 39
- expand_index: int32 [16, 2048, 2], P('row', 'col'), may hold values from 0 to 143
- doc_lengths: int32 [16, 8], P('row'), may hold values from 1 to 1024, 2048 in all within a row
Outputs:
- memory_out: bfloat16 [16, 2048, 2560], P('row', 'col')
- new_table: float32 [10240, 1280], P(('row', 'col'))
- new_moment: float32 [10240, 1280], P(('row', 'col'))
- new_second: float32 [10240, 1280], P(('row', 'col'))
Inputs may be any that keep to these rules, and one draw needn't show every extreme that they name: `row_owner`: among the 144 slots of one device's row list no owner is named more than 2 times, a bound that some block reaches. `doc_lengths`: the 8 lengths of a sequence sum to 2048; the largest is exactly 1024.
All inputs are finite; a program needn't handle non-finite values.
Results may differ from a plain program's by a relative error of at most 0.009.
Values may be sent and summed in bfloat16 or wider, within the bound.
A program may use at most 64 MiB of HBM per device.

v0:
```python
import jax
import jax.numpy as jnp
from jax import lax
from jax.sharding import PartitionSpec as P

DILATION_STEP = 3


NORM_EPS = 1e-06
BETA_ONE = 0.9
BETA_TWO = 0.95
ADAM_EPS = 1e-08
LEARN_RATE = 0.01
DECAY_RATE = 0.1
STEP_COUNT = 10.0


def from_behind(value, axis, steps):
    count = lax.axis_size(axis)
    first, last = (max(0, -steps), min(count, count - steps))
    return lax.ppermute(value, axis, [(source, source + steps) for source in range(first, last)])


def rms_scale(values):
    return lax.rsqrt(jnp.mean(values * values, axis=-1, keepdims=True) + NORM_EPS)


def doc_index(positions, lengths):
    doc_ends = jnp.cumsum(lengths, dtype=jnp.int32)
    return jnp.sum((positions[:, None] >= doc_ends[None, :-1]).astype(jnp.int32), axis=1)


def adamw_update(current, moment, second, gradient):
    moment_new = BETA_ONE * moment + (1.0 - BETA_ONE) * gradient
    second_new = BETA_TWO * second + (1.0 - BETA_TWO) * gradient * gradient
    first_hat = moment_new / (1.0 - BETA_ONE**STEP_COUNT)
    second_hat = second_new / (1.0 - BETA_TWO**STEP_COUNT)
    updated = current - LEARN_RATE * (
        first_hat / (jnp.sqrt(second_hat) + ADAM_EPS) + DECAY_RATE * current
    )
    return (updated, moment_new, second_new)


def contract_last(left, right):
    return lax.dot_general(
        left, right, (((1,), (1,)), ((), ())), preferred_element_type=jnp.float32
    )


def contract_first(left, right):
    return lax.dot_general(
        left, right, (((0,), (0,)), ((), ())), preferred_element_type=jnp.float32
    )


def on_device(
    hidden,
    grad_out,
    w_key,
    w_value,
    depthwise_weight,
    table,
    adam_m,
    adam_v,
    row_owner,
    row_local,
    expand_index,
    doc_lengths,
):
    n_rows = lax.axis_size("row")
    n_cols = lax.axis_size("col")
    n_devices = n_rows * n_cols
    tok_count = hidden.shape[1]
    model_width = hidden.shape[2]
    row_width = w_key.shape[0] * n_rows
    slot_count = row_owner.shape[1]
    rows_dev = table.shape[0]
    kernel_taps = depthwise_weight.shape[0]
    border_rows = DILATION_STEP * (kernel_taps - 1)
    capacity = max(2, 4 * slot_count // (3 * n_devices))
    buffer_slots = n_devices * capacity
    root_width = jnp.sqrt(jnp.float32(model_width))
    owners = row_owner[0, :, 0]
    locals_in = row_local[0]
    slot_iota = jnp.arange(slot_count, dtype=jnp.int32)
    same_owner = (owners[:, None] == owners[None, :]) & (slot_iota[None, :] < slot_iota[:, None])
    rank = jnp.sum(same_owner.astype(jnp.int32), axis=1)
    slot_place = owners * capacity + rank
    buffer_iota = jnp.arange(buffer_slots, dtype=jnp.int32)
    placed = buffer_iota[:, None] == slot_place[None, :]
    request = jnp.sum(jnp.where(placed, locals_in[None, :] + 1, 0), axis=1) - 1
    request = request.reshape(n_rows, n_cols, capacity)
    arrived = lax.all_to_all(
        lax.all_to_all(request, "row", split_axis=0, concat_axis=0, tiled=True),
        "col",
        split_axis=1,
        concat_axis=1,
        tiled=True,
    )
    arrived_flat = arrived.reshape(buffer_slots)
    owned_iota = jnp.arange(rows_dev, dtype=jnp.int32)
    table16 = table.astype(jnp.bfloat16)
    serve = (arrived_flat[:, None] == owned_iota[None, :]).astype(jnp.bfloat16)
    reply = jnp.dot(serve, table16, preferred_element_type=jnp.float32).astype(jnp.bfloat16)
    reply = reply.reshape(n_rows, n_cols, capacity, row_width)
    fetched = lax.all_to_all(
        lax.all_to_all(reply, "row", split_axis=0, concat_axis=0, tiled=True),
        "col",
        split_axis=1,
        concat_axis=1,
        tiled=True,
    )
    fetched = fetched.reshape(buffer_slots, row_width)
    token_place = jnp.take(slot_place, expand_index[0])
    spread = jnp.zeros((tok_count, buffer_slots), jnp.int32)
    for lookup in range(token_place.shape[1]):
        spread = spread + (token_place[:, lookup][:, None] == buffer_iota[None, :]).astype(
            jnp.int32
        )
    spread = spread.astype(jnp.bfloat16)
    memory = jnp.dot(spread, fetched, preferred_element_type=jnp.float32).astype(jnp.bfloat16)
    key_full, value_full = (
        lax.all_gather(w_key, "row", axis=0, tiled=True),
        lax.all_gather(w_value, "row", axis=0, tiled=True),
    )
    key = jnp.dot(memory, key_full, preferred_element_type=jnp.float32)
    value = jnp.dot(memory, value_full, preferred_element_type=jnp.float32)
    key_scale = rms_scale(key)
    key_norm = key * key_scale
    hidden_f = hidden[0].astype(jnp.float32)
    hidden_norm = hidden_f * rms_scale(hidden_f)
    gate = jax.nn.sigmoid(jnp.sum(hidden_norm * key_norm, axis=-1, keepdims=True) / root_width)
    gated = (gate * value).astype(jnp.bfloat16)
    gated_f = gated.astype(jnp.float32)
    gated_scale = rms_scale(gated_f)
    gated_normalized = gated_f * gated_scale
    lengths = doc_lengths[0]
    first_pos = lax.axis_index("col") * tok_count
    earlier = from_behind(gated[tok_count - border_rows :], "col", 1)
    extended = jnp.concatenate([earlier, gated], axis=0).astype(jnp.float32)
    extended_norm = extended * rms_scale(extended)
    pos_before = first_pos - border_rows + jnp.arange(tok_count + border_rows, dtype=jnp.int32)
    doc_before = doc_index(pos_before, lengths)
    doc_here = doc_before[border_rows:]
    convolved_rows = jnp.zeros((tok_count, model_width), jnp.float32)
    for kernel_tap_index in range(kernel_taps):
        shift_amount = kernel_tap_index * DILATION_STEP
        source_pos = pos_before[border_rows - shift_amount : border_rows - shift_amount + tok_count]
        source_doc = doc_before[border_rows - shift_amount : border_rows - shift_amount + tok_count]
        same_doc = ((source_pos >= 0) & (source_doc == doc_here)).astype(jnp.float32)[:, None]
        convolved_rows = (
            convolved_rows
            + depthwise_weight[kernel_tap_index]
            * extended_norm[border_rows - shift_amount : border_rows - shift_amount + tok_count]
            * same_doc
        )
    memory_out = (jax.nn.silu(convolved_rows) + gated_f).astype(jnp.bfloat16)
    grad_f = grad_out[0].astype(jnp.float32)
    sig = jax.nn.sigmoid(convolved_rows)
    convolution_gradient = grad_f * sig * (1.0 + convolved_rows * (1.0 - sig))
    next_rows = from_behind(
        convolution_gradient[:border_rows].astype(jnp.bfloat16), "col", -1
    ).astype(jnp.float32)
    grad_ext = jnp.concatenate([convolution_gradient, next_rows], axis=0)
    pos_after = first_pos + jnp.arange(tok_count + border_rows, dtype=jnp.int32)
    doc_after = doc_index(pos_after, lengths)
    normalized_gradient = jnp.zeros((tok_count, model_width), jnp.float32)
    for kernel_tap_index in range(kernel_taps):
        shift_amount = kernel_tap_index * DILATION_STEP
        same_doc = (
            doc_after[shift_amount : shift_amount + tok_count] == doc_after[:tok_count]
        ).astype(jnp.float32)[:, None]
        normalized_gradient = normalized_gradient + depthwise_weight[kernel_tap_index] * (
            grad_ext[shift_amount : shift_amount + tok_count] * same_doc
        )
    gated_grad = grad_f + gated_scale * (
        normalized_gradient
        - gated_normalized
        * jnp.mean(gated_normalized * normalized_gradient, axis=-1, keepdims=True)
    )
    value_grad = gated_grad * gate
    score_grad = gate * (1.0 - gate) * jnp.sum(gated_grad * value, axis=-1, keepdims=True)
    target = score_grad * hidden_norm / root_width
    key_grad = key_scale * (target - key_norm * jnp.mean(key_norm * target, axis=-1, keepdims=True))
    key_grad16 = key_grad.astype(jnp.bfloat16)
    value_grad16 = value_grad.astype(jnp.bfloat16)
    memory_grad = (
        contract_last(key_grad16, key_full) + contract_last(value_grad16, value_full)
    ).astype(jnp.bfloat16)
    slot_grad = contract_first(spread, memory_grad)
    gradients = lax.all_to_all(
        lax.all_to_all(
            slot_grad.reshape(n_rows, n_cols, capacity, row_width).astype(jnp.bfloat16),
            "row",
            split_axis=0,
            concat_axis=0,
            tiled=True,
        ),
        "col",
        split_axis=1,
        concat_axis=1,
        tiled=True,
    ).astype(jnp.float32)
    gradients = gradients.reshape(buffer_slots, row_width)
    picker = (owned_iota[:, None] == arrived_flat[None, :]).astype(jnp.float32)
    row_grad = jnp.dot(
        picker, gradients, precision=lax.Precision.HIGHEST, preferred_element_type=jnp.float32
    )
    new_table, new_moment, new_second = adamw_update(table, adam_m, adam_v, row_grad)
    return (memory_out[None], new_table, new_moment, new_second)


def solution(mesh):
    placed = (
        P("row", "col", None),
        P("row", "col", None),
        P("row", None),
        P("row", None),
        P(),
        P(("row", "col"), None),
        P(("row", "col"), None),
        P(("row", "col"), None),
        P("row", "col", None),
        P("row", "col"),
        P("row", "col", None),
        P("row", None),
    )
    return jax.shard_map(
        on_device,
        mesh=mesh,
        in_specs=placed,
        out_specs=(
            P("row", "col", None),
            P(("row", "col"), None),
            P(("row", "col"), None),
            P(("row", "col"), None),
        ),
        check_vma=False,
    )
```

profile of v0, /device:TPU:1, one launch (start us, length us, event | category | flops | bytes accessed | tf_op | source)
XLA Modules:
  0.0 245.8 jit_solution(2760345287618477085)
XLA Ops:
  11.4 17.1 %all_to_all.30 = s32[16,16,2]{1,2,0:T(2,128)S(1)} all-to-all(s32[16,16,2]{1,2,0:T(2,128)S(1)} %copy.47), channel_id=1, replica_groups=mesh['row'=16,'col'=16] {'row'}, dimensions={0} | all-to-all | bytes 4096 | tf_op jit(solution)/shard_map/all_to_all | solution.py:94
  28.6 13.0 %all_to_all.31 = s32[16,16,2]{0,2,1:T(2,128)S(1)} all-to-all(s32[16,16,2]{0,2,1:T(2,128)S(1)} %copy.48), channel_id=1, replica_groups=mesh['row'=16,'col'=16] {'col'}, dimensions={1} | all-to-all | bytes 4096 | tf_op jit(solution)/shard_map/all_to_all | solution.py:93
  42.5 1.4 reshape.158
  43.9 5.4 %all-to-all-start.2 = ((bf16[16,16,2,1280]{3,2,1,0:T(2,128)(2,1)}), bf16[16,16,2,1280]{3,2,1,0:T(2,128)(2,1)S(1)}, u32[]{:S(2)}, u32[]{:S(2)}) async-start(bf16[16,16,2,1280]{3,2,1,0:T(2,128)(2,1)} %reshape.158), calls=%async_computation.2 | async-start | bytes 2621440 | tf_op jit(solution)/shard_map/all_to_all | solution.py:107
  49.7 1.9 gather_fusion
  52.0 36.2 %all-to-all-done.2 = bf16[16,16,2,1280]{3,2,1,0:T(2,128)(2,1)S(1)} async-done(((bf16[16,16,2,1280]{3,2,1,0:T(2,128)(2,1)}), bf16[16,16,2,1280]{3,2,1,0:T(2,128)(2,1)S(1)}, u32[]{:S(2)}, u32[]{:S(2)}) %all-to-all-start.2) | async-done | bytes 1310752 | tf_op jit(solution)/shard_map/all_to_all | solution.py:107
  88.2 2.3 copy.50
  90.5 6.7 %all-to-all-start.3 = ((bf16[16,16,2,1280]{3,2,0,1:T(2,128)(2,1)}), bf16[16,16,2,1280]{3,2,0,1:T(2,128)(2,1)S(1)}, u32[]{:S(2)}, u32[]{:S(2)}) async-start(bf16[16,16,2,1280]{3,2,0,1:T(2,128)(2,1)} %copy.50), calls=%async_computation.3 | async-start | bytes 2621440 | tf_op jit(solution)/shard_map/all_to_all | solution.py:106
  97.9 17.6 %all-to-all-done.3 = bf16[16,16,2,1280]{3,2,0,1:T(2,128)(2,1)S(1)} async-done(((bf16[16,16,2,1280]{3,2,0,1:T(2,128)(2,1)}), bf16[16,16,2,1280]{3,2,0,1:T(2,128)(2,1)S(1)}, u32[]{:S(2)}, u32[]{:S(2)}) %all-to-all-start.3) | async-done | bytes 1310752 | tf_op jit(solution)/shard_map/all_to_all | solution.py:106
  115.5 1.2 copy.51
  117.6 4.1 %multiply_reduce_fusion.1 = (f32[128]{0:T(128)S(1)}, f32[128,2560]{1,0:T(8,128)S(1)}) fusion(bf16[128,1280]{1,0:T(8,128)(2,1)S(1)} %convolution_convert_fusion.2, bf16[1280,2560]{1,0:T(8,128)(2,1)} %all-gather.3.cloned.1.call-done), kind=kOutput, calls=%fused_computation.65 | convolution fusion | flops 839516032 | bytes 8192512 | tf_op jit(solution)/shard_map/dot_general | solution.py:126
  122.1 14.3 %all-gather.5.cloned.1.call-done = bf16[1280,2560]{1,0:T(8,128)(2,1)} async-done(((bf16[80,2560]{1,0:T(8,128)(2,1)}), bf16[1280,2560]{1,0:T(8,128)(2,1)}) %all-gather.5.cloned.1.call-update) | async-done | bytes 6553616 | tf_op jit(solution)/shard_map/all_gather | solution.py:124
  136.5 4.0 %fusion.28 = (f32[128]{0:T(128)S(1)}, bf16[128,2560]{1,0:T(8,128)(2,1)S(1)}, f32[128,2560]{1,0:T(8,128)S(1)}) fusion(f32[128]{0:T(128)S(1)} %add_divide_fusion.1, bf16[128,1280]{1,0:T(8,128)(2,1)S(1)} %convolution_convert_fusion.2, bf16[1280,2560]{1,0:T(8,128)(2,1)} %all-gather.5.cloned.1.call-done), kind=kOutput, calls=%fused_computation.46 | convolution fusion | flops 840499072 | bytes 8848384 | tf_op jit(solution)/shard_map/dot_general | solution.py:127
  140.5 3.1 %collective-permute-start = (bf16[9,2560]{1,0:T(8,128)(2,1)S(1)}, bf16[9,2560]{1,0:T(8,128)(2,1)S(1)}, u32[]{:S(2)}, u32[]{:S(2)}) collective-permute-start(bf16[9,2560]{1,0:T(8,128)(2,1)S(1)} %slice.128), channel_id=1, source_target_pairs={{0,1},{1,2},{2,3},{3,4},{4,5},{5,6},{6,7},{7,8},{8,9},{9,10},{10,1... | collective-permute-start | bytes 138248 | tf_op jit(solution)/shard_map/ppermute | solution.py:21
  143.8 1.3 collective-permute-done
  145.8 1.2 fusion.26
  147.0 1.5 collective-permute-start.1
  148.5 4.5 %collective-permute-done.1 = bf16[9,2560]{1,0:T(8,128)(2,1)S(1)} collective-permute-done((bf16[9,2560]{1,0:T(8,128)(2,1)S(1)}, bf16[9,2560]{1,0:T(8,128)(2,1)S(1)}, u32[]{:S(2)}, u32[]{:S(2)}) %collective-permute-start.1) | collective-permute-done | bytes 46112 | tf_op jit(solution)/shard_map/ppermute | solution.py:21
  154.3 1.8 multiply_reduce_fusion
  156.6 3.0 %fusion.38 = f32[128,1280]{1,0:T(8,128)} fusion(bf16[1280,2560]{1,0:T(8,128)(2,1)S(1)} %bitcast.43, f32[128,2560]{1,0:T(8,128)S(1)} %get-tuple-element.31, bf16[1,128,2560]{2,1,0:T(8,128)(2,1)S(1)} %copy-done.1, f32[128]{0:T(128)S(1)} %broadcast_multiply_fusion, f32[128]{0:T(128)S(1)} %fusion.59, f32[128]{0:T(128)S(1)} %add_rsqrt_fusion.2, ...), kind=kOutput, calls=%fused_computation.67 | convolution fusion | flops 841809920 | bytes 9177088 | tf_op jit(solution)/shard_map/dot_general | solution.py:45
  159.7 6.0 %convolution_convert_fusion.1 = bf16[512,1280]{1,0:T(8,128)(2,1)S(1)} fusion(f32[128,1280]{1,0:T(8,128)} %fusion.38, bf16[1280,2560]{1,0:T(8,128)(2,1)} %all-gather.5.cloned.1.call-done, f32[128]{0:T(128)S(1)} %add_divide_fusion.1, f32[128,2560]{1,0:T(8,128)S(1)} %get-tuple-element.16, bf16[128,2560]{1,0:T(8,128)(2,1)S(1)} %get-tuple-element.18, ...), kind=kOutput, calls=%fused_computation.2 | convolution fusion | flops 1010958336 | bytes 11143680 | tf_op jit(solution)/shard_map/dot_general | solution.py:51
  166.2 40.2 %all_to_all.32 = bf16[16,16,2,1280]{3,2,1,0:T(2,128)(2,1)S(1)} all-to-all(bf16[16,16,2,1280]{3,2,1,0:T(2,128)(2,1)S(1)} %convert_element_type.126), channel_id=1, replica_groups=mesh['row'=16,'col'=16] {'row'}, dimensions={0} | all-to-all | bytes 2621440 | tf_op jit(solution)/shard_map/all_to_all | solution.py:192
  207.6 27.9 %all_to_all.33 = bf16[16,16,2,1280]{3,2,0,1:T(2,128)(2,1)S(1)} all-to-all(bf16[16,16,2,1280]{3,2,0,1:T(2,128)(2,1)S(1)} %copy.52), channel_id=1, replica_groups=mesh['row'=16,'col'=16] {'col'}, dimensions={1} | all-to-all | bytes 2621440 | tf_op jit(solution)/shard_map/all_to_all | solution.py:191
  237.7 1.2 multiply_subtract_fusion
  (77 shorter events, 14.3 us)
Async XLA Ops:
  7.2 34.8 %copy-start.3 = (f32[40,1280]{1,0:T(8,128)S(1)}, f32[40,1280]{1,0:T(8,128)}, u32[]{:S(2)}) copy-start(f32[40,1280]{1,0:T(8,128)} %param.17) | copy-start | bytes 614404
  7.2 110.5 %all-gather.3.cloned.1.call-start = ((), (), s32[]{:S(2)}) async-start(), calls=%async_computation.6 | async-start | bytes 6963200 | tf_op jit(solution)/shard_map/all_gather | solution.py:123
  7.9 128.6 %all-gather.5.cloned.1.call-start = ((), (), s32[]{:S(2)}) async-start(), calls=%async_computation.7 | async-start | bytes 6963200 | tf_op jit(solution)/shard_map/all_gather | solution.py:124
  43.9 5.5 %copy-start.7 = (s32[1,128,2]{1,2,0:T(2,128)S(1)}, s32[1,128,2]{1,2,0:T(2,128)}, u32[]{:S(2)}) copy-start(s32[1,128,2]{1,2,0:T(2,128)} %param.22) | copy-start | bytes 3076
  43.9 44.3 %all-to-all-start.2 = ((bf16[16,16,2,1280]{3,2,1,0:T(2,128)(2,1)}), bf16[16,16,2,1280]{3,2,1,0:T(2,128)(2,1)S(1)}, u32[]{:S(2)}, u32[]{:S(2)}) async-start(bf16[16,16,2,1280]{3,2,1,0:T(2,128)(2,1)} %reshape.158), calls=%async_computation.2 | async-start | bytes 2621440 | tf_op jit(solution)/shard_map/all_to_all | solution.py:107
  49.7 2.1 copy-start.8
  90.5 7.0 %copy-start = (bf16[1,128,2560]{2,1,0:T(8,128)(2,1)S(1)}, bf16[1,128,2560]{2,1,0:T(8,128)(2,1)}, u32[]{:S(2)}) copy-start(bf16[1,128,2560]{2,1,0:T(8,128)(2,1)} %param.12) | copy-start | bytes 1966084
  90.5 24.9 %all-to-all-start.3 = ((bf16[16,16,2,1280]{3,2,0,1:T(2,128)(2,1)}), bf16[16,16,2,1280]{3,2,0,1:T(2,128)(2,1)S(1)}, u32[]{:S(2)}, u32[]{:S(2)}) async-start(bf16[16,16,2,1280]{3,2,0,1:T(2,128)(2,1)} %copy.50), calls=%async_computation.3 | async-start | bytes 2621440 | tf_op jit(solution)/shard_map/all_to_all | solution.py:106
  122.1 21.5 %copy-start.6 = (f32[4,2560]{1,0:T(4,128)S(1)}, f32[4,2560]{1,0:T(4,128)}, u32[]{:S(2)}) copy-start(f32[4,2560]{1,0:T(4,128)} %param.16) | copy-start | bytes 122884
  140.5 4.6 %collective-permute-start = (bf16[9,2560]{1,0:T(8,128)(2,1)S(1)}, bf16[9,2560]{1,0:T(8,128)(2,1)S(1)}, u32[]{:S(2)}, u32[]{:S(2)}) collective-permute-start(bf16[9,2560]{1,0:T(8,128)(2,1)S(1)} %slice.128), channel_id=1, source_target_pairs={{0,1},{1,2},{2,3},{3,4},{4,5},{5,6},{6,7},{7,8},{8,9},{9,10},{10,1... | collective-permute-start | bytes 138248 | tf_op jit(solution)/shard_map/ppermute | solution.py:21
  143.8 2.0 copy-start.2
  145.8 10.8 %slice-start = ((s8[6553600]{0:T(1024)(128)(4,1)}), s8[4194304]{0:T(1024)(128)(4,1)S(1)}, s32[]{:S(2)}) async-start(s8[6553600]{0:T(1024)(128)(4,1)} %bitcast.42), calls=%async_computation.8 | async-start | bytes 8388608
  147.0 6.0 %collective-permute-start.1 = (bf16[9,2560]{1,0:T(8,128)(2,1)S(1)}, bf16[9,2560]{1,0:T(8,128)(2,1)S(1)}, u32[]{:S(2)}, u32[]{:S(2)}) collective-permute-start(bf16[9,2560]{1,0:T(8,128)(2,1)S(1)} %slice.214), channel_id=1, source_target_pairs={{1,0},{2,1},{3,2},{4,3},{5,4},{6,5},{7,6},{8,7},{9,8},{10,9},{11,1... | collective-permute-start | bytes 138248 | tf_op jit(solution)/shard_map/ppermute | solution.py:21
  153.1 3.5 %slice-start.1 = ((s8[6553600]{0:T(1024)(128)(4,1)}), s8[2359296]{0:T(1024)(128)(4,1)S(1)}, s32[]{:S(2)}) async-start(s8[6553600]{0:T(1024)(128)(4,1)} %bitcast.42), calls=%async_computation.9 | async-start | bytes 4718592
  154.3 1.8 copy-start.1
  236.7 0.9 copy-start.4
  236.7 1.0 copy-start.5
Sparse Core Ops, SparseCore 0:
  9.8 69.3 all-gather.2
  81.1 55.3 all-gather.4
where the time goes:
time: 246 us
  blocking collectives  98.2 us (40%)
  waiting for transfers between devices  75.4 us (31%)
  matrix products  19.2 us (8%)
  starting transfers between devices  16.8 us (7%)
  between operations  14.4 us (6%)
  local copies, waits for them, and re-layouts  12.9 us (5%)
  other arithmetic  8.87 us (4%)
    all_to_all x1, blocking collectives, on_device(): lax.all_to_all(slot_grad.reshape(n_rows, n_cols, capacity, row_width).ast...  40.2 us
    all_to_all x1, waiting for transfers between devices, on_device(): lax.all_to_all(reply, 'row', split_axis=0, concat_axis=0, tiled=True)  36.2 us
    all_to_all x1, blocking collectives, on_device(): lax.all_to_all(lax.all_to_all(slot_grad.reshape(n_rows, n_cols, capacity,...  27.9 us
    all_to_all x1, waiting for transfers between devices, on_device(): lax.all_to_all(lax.all_to_all(reply, 'row', split_axis=0, concat_axis=0,...  17.6 us
    all_to_all x1, blocking collectives, on_device(): lax.all_to_all(request, 'row', split_axis=0, concat_axis=0, tiled=True)  17.1 us
    all_gather x1, waiting for transfers between devices, on_device(): lax.all_gather(w_value, 'row', axis=0, tiled=True)  14.3 us
    all_to_all x1, blocking collectives, on_device(): lax.all_to_all(lax.all_to_all(request, 'row', split_axis=0, concat_axis=0...  13 us
    all_to_all x1, starting transfers between devices, on_device(): lax.all_to_all(lax.all_to_all(reply, 'row', split_axis=0, concat_axis=0,...  6.65 us
  transfers between devices with their start and end apart: 6, of which 5 were waited for; matrix products, arithmetic and copies ran while one was open for 7% of the time, Pallas kernels for 0%

commit v1 on v0

v1 whole, which is shorter than its diff:
```python
import jax
import jax.numpy as jnp
from jax import lax
from jax.experimental import pallas as pl
from jax.experimental.pallas import tpu as pltpu
from jax.sharding import PartitionSpec as P

DILATION_STEP = 3
NORM_EPS = 1e-06
BETA_ONE = 0.9
BETA_TWO = 0.95
ADAM_EPS = 1e-08
LEARN_RATE = 0.01
DECAY_RATE = 0.1
STEP_COUNT = 10.0

Z, X, Y = 8, 4, 4
PLANE = 2 * X * Y
D, E = 2560, 1280
TOK, U, R_DEV = 128, 144, 40
HALF = E // 2
TROWS = 48
MSG = 2 * Z
PLACES = PLANE * MSG
CB = 512
NB = 2 * D // CB
WROWS = 80

MESH = pl.DeviceIdType.MESH
F32, BF16, I32 = jnp.float32, jnp.bfloat16, jnp.int32


class Here:
    def __init__(self):
        self.row = lax.axis_index("row")
        self.col = lax.axis_index("col")
        self.z = self.row // 2
        self.core = self.row % 2
        self.x = self.col // Y
        self.y = self.col % Y
        self.plane = self.core * (X * Y) + self.col

    def mate(self, i):
        q = lax.rem(self.plane + i, PLANE)
        return q, (self.z * 2 + q // (X * Y), q % (X * Y))

    def zed(self, step):
        return lax.rem(self.z + step + Z, Z)

    def at_z(self, step):
        return (self.zed(step) * 2 + self.core, self.col)

    def exx(self, step):
        return lax.rem(self.x + step + X, X)

    def wye(self, step):
        return lax.rem(self.y + step + Y, Y)

    def at_x(self, step):
        return (self.row, self.exx(step) * Y + self.y)

    def at_y(self, step):
        return (self.row, self.x * Y + self.wye(step))

    def partner(self):
        return (self.z * 2 + 1 - self.core, self.col)


def remote(src, dst, send, recv, device):
    return pltpu.make_async_remote_copy(
        src_ref=src, dst_ref=dst, send_sem=send, recv_sem=recv, device_id=device, device_id_type=MESH
    )


def greet(here):
    barrier = pltpu.get_barrier_semaphore()

    def one(i, carry):
        _, device = here.mate(i)
        pl.semaphore_signal(barrier, inc=1, device_id=device, device_id_type=MESH)
        return carry

    lax.fori_loop(1, PLANE, one, 0)
    for step in (1, -1):
        pl.semaphore_signal(barrier, inc=1, device_id=here.at_z(step), device_id_type=MESH)
    return lambda: pl.semaphore_wait(barrier, PLANE + 1)


def iota(shape, dim):
    return lax.broadcasted_iota(I32, shape, dim)


def one_hot(mask):
    return jnp.where(mask, 1.0, 0.0).astype(BF16)


def plan_slots(owner_ref, local_ref, expand_ref, spread, req_out):
    owner_c = owner_ref[...]
    eye = iota((U, U), 0) == iota((U, U), 1)
    owner_r = jnp.sum(jnp.where(eye, owner_c, 0), axis=0, keepdims=True)
    local_c = jnp.sum(jnp.where(eye, local_ref[...], 0), axis=1, keepdims=True)
    before = (owner_c == owner_r) & (iota((U, U), 1) < iota((U, U), 0))
    rank_c = jnp.sum(jnp.where(before, 1, 0), axis=1, keepdims=True)
    k_c = (owner_c >> 5) * 2 + rank_c
    place_c = (owner_c & 31) * MSG + k_c
    mates = one_hot((owner_r & 31) == iota((PLANE, U), 0))
    wanted = jnp.where(k_c == iota((U, 128), 1), local_c + 1, 0).astype(F32).astype(BF16)
    request = jnp.dot(mates, wanted, preferred_element_type=F32)
    for q in range(PLANE):
        req_out[q] = request[q : q + 1, :]
    expand = expand_ref[...]
    reads = jnp.zeros((TOK, U), F32)
    for lookup in range(2):
        reads = reads + jnp.where(expand[:, lookup : lookup + 1] == iota((TOK, U), 1), 1.0, 0.0)
    places = one_hot(place_c == iota((U, PLACES), 1))
    spread[...] = jnp.dot(reads.astype(BF16), places, preferred_element_type=F32).astype(BF16)


def plan_serve(req_in, serve):
    asked = req_in[:, 0, :].astype(BF16)
    owner_rows = one_hot(iota((PLACES, PLANE), 0) // MSG == iota((PLACES, PLANE), 1))
    wide = jnp.dot(owner_rows, asked, preferred_element_type=F32)
    k = iota((PLACES, 128), 0) % MSG
    value = jnp.sum(jnp.where(k == iota((PLACES, 128), 1), wide, 0.0), axis=1, keepdims=True)
    zed = (iota((PLACES, 1), 0) % MSG) // 2
    target = jnp.where(value > 0.5, zed * TROWS + value.astype(I32) - 1, -1)
    serve[...] = one_hot(target == iota((PLACES, Z * TROWS), 1))


def send_mates(here, src, dst, send, recv):
    def one(i, carry):
        q, device = here.mate(i)
        remote(src.at[q], dst.at[here.plane], send, recv, device).start()
        return carry

    lax.fori_loop(1, PLANE, one, 0)


def mates_arrived(here, dst, recv):
    ref = dst.at[pl.ds(0, PLANE - 1)]
    pltpu.make_async_copy(ref, ref, recv).wait()


def mates_sent(here, src, send):
    ref = src.at[pl.ds(0, PLANE - 1)]
    pltpu.make_async_copy(ref, ref, send).wait()


class Ring:
    def __init__(self, here, block, send, recv, far):
        self.here, self.block, self.send, self.recv, self.far = here, block, send, recv, far

    def copy(self, way, step):
        sign = 1 if way == 0 else -1
        ref = self.block(self.here.zed(-sign * (step - 1)))
        return remote(ref, ref, self.send.at[way, step - 1], self.recv.at[way, step - 1], self.here.at_z(sign))

    def steps(self, way):
        return Z // 2 if way == self.far else Z // 2 - 1

    def start(self, step):
        for way in range(2):
            if step <= self.steps(way):
                self.copy(way, step).start()

    def arrived(self, step):
        got = []
        for way in range(2):
            if step <= self.steps(way):
                sign = 1 if way == 0 else -1
                ref = self.block(self.here.zed(-sign * step))
                remote(ref, ref, self.send.at[way, step - 1], self.recv.at[way, step - 1], self.here.at_z(-sign)).wait_recv()
                got.append(-sign * step)
        return got

    def drain(self):
        for way in range(2):
            for step in range(1, self.steps(way) + 1):
                self.copy(way, step).wait_send()


class Cross:
    def __init__(self, here, axis, weights, base, send, recv):
        self.here, self.weights, self.base, self.send, self.recv = here, weights, base, send, recv
        self.at = here.at_x if axis == "x" else here.at_y
        self.place = here.exx if axis == "x" else here.wye

    def copy(self, way, zz, i):
        sign = 1 if way % 2 == 0 else -1
        if way < 2:
            ref = self.weights.at[self.base + self.place(0), zz, self.here.core]
        else:
            ref = self.weights.at[self.base + self.place(-sign), zz, self.here.core, :, pl.ds((way - 2) * (CB // 2), CB // 2)]
        return remote(ref, ref, self.send.at[way, i], self.recv.at[way, i], self.at(sign))

    def got(self, way, zz, i):
        sign = 1 if way % 2 == 0 else -1
        if way < 2:
            ref = self.weights.at[self.base + self.place(-sign), zz, self.here.core]
        else:
            ref = self.weights.at[
                self.base + self.place(-2 * sign), zz, self.here.core, :, pl.ds((way - 2) * (CB // 2), CB // 2)
            ]
        return remote(ref, ref, self.send.at[way, i], self.recv.at[way, i], self.at(-sign))

    def start(self, zz, i):
        for way in (0, 1):
            self.copy(way, zz, i).start()

    def relay(self, zz, i):
        for way in (0, 1):
            self.got(way, zz, i).wait_recv()
            self.copy(way + 2, zz, i).start()

    def finish(self, zz, i):
        for way in (2, 3):
            self.got(way, zz, i).wait_recv()

    def drain(self, zz, i):
        for way in range(4):
            self.copy(way, zz, i).wait_send()


def gather_kernel(
    owner_ref, local_ref, expand_ref, table_ref, wk_ref, wv_ref,
    memory_ref, spread_ref, serve_ref, key_ref, value_ref,
    weights, tab, req_out, req_in, reply, fetched,
    load_sem, store_sem, req_send, req_recv, rep_send, rep_recv, tz_send, tz_recv, wz_send, wz_recv,
    xy_send, xy_recv, core_send, core_recv,
):
    here = Here()
    greeted = greet(here)
    loads = []
    for b in range(NB):
        src = wk_ref if b < NB // 2 else wv_ref
        loads.append(
            pltpu.make_async_copy(
                src.at[:, pl.ds((b % (NB // 2)) * CB, CB)], weights.at[b, here.z, here.core], load_sem.at[b]
            )
        )
        loads[-1].start()
    for h in range(2):
        tab[h, here.z, 0:R_DEV, :] = table_ref[:, h * HALF : (h + 1) * HALF].astype(BF16)
        tab[h, here.z, R_DEV:TROWS, :] = jnp.zeros((TROWS - R_DEV, HALF), BF16)
    plan_slots(owner_ref, local_ref, expand_ref, spread_ref, req_out)
    greeted()

    tables = [Ring(here, lambda zz, h=h: tab.at[h, zz], tz_send.at[h], tz_recv.at[h], h) for h in range(2)]
    for ring in tables:
        ring.start(1)
    send_mates(here, req_out, req_in, req_send, req_recv)
    req_in[here.plane] = req_out[here.plane]
    for load in loads:
        load.wait()
    crosses = [
        Cross(here, "x", weights, 0, xy_send.at[0], xy_recv.at[0]),
        Cross(here, "y", weights, NB // 2, xy_send.at[1], xy_recv.at[1]),
    ]
    order = [0, -1, 1, -2, 2, -3, 3, 4]
    zeds = [here.zed(step) for step in order]
    for step in (2, 3, 4):
        for ring in tables:
            ring.arrived(step - 1)
            ring.start(step)
    blocks = [here.x, NB // 2 + here.y, NB // 2 - 1, NB - 1]
    pieces = [
        Ring(here, lambda zz, b=b: weights.at[b, zz, here.core], wz_send.at[i], wz_recv.at[i], i % 2)
        for i, b in enumerate(blocks)
    ]
    for ring in pieces[:2]:
        ring.start(1)
    mates_arrived(here, req_in, req_recv)
    plan_serve(req_in, serve_ref)
    for h in range(2):
        tables[h].arrived(4)
        rows = jnp.dot(serve_ref[...], tab[h].reshape(Z * TROWS, HALF), preferred_element_type=F32)
        reply[h] = rows.astype(BF16).reshape(PLANE, MSG, HALF)
        fetched[h, here.plane] = reply[h, here.plane]
        send_mates(here, reply.at[h], fetched.at[h], rep_send.at[h], rep_recv.at[h])
    seen = 1
    relayed = 1
    for step in (1, 2, 3, 4):
        for ring in pieces[:2]:
            ring.arrived(step)
            if step < 4:
                ring.start(step + 1)
        if step == 3:
            for ring in pieces[2:]:
                ring.start(1)
        upto = min(Z, seen + 2)
        for i in range(seen, upto):
            for cross in crosses:
                cross.start(zeds[i], i)
        for i in range(relayed, seen):
            for cross in crosses:
                cross.relay(zeds[i], i)
        relayed, seen = seen, upto
    for i in range(relayed, Z):
        for cross in crosses:
            cross.relay(zeds[i], i)

    def to_partner(b):
        ref = weights.at[b, :, here.core]
        return remote(ref, ref, core_send.at[b], core_recv.at[b], here.partner())

    for b in (here.x, NB // 2 + here.y):
        to_partner(b).start()
    for step in (-1, 1):
        to_partner(here.exx(step)).start()
        to_partner(NB // 2 + here.wye(step)).start()
    for step in (1, 2, 3, 4):
        for ring in pieces[2:]:
            ring.arrived(step)
            if step < 4:
                ring.start(step + 1)
    for b in (NB // 2 - 1, NB - 1):
        to_partner(b).start()
    for i in range(1, Z):
        for cross in crosses:
            cross.finish(zeds[i], i)
    to_partner(here.exx(2)).start()
    to_partner(NB // 2 + here.wye(2)).start()
    for h in range(2):
        mates_arrived(here, fetched.at[h], rep_recv.at[h])
        memory_ref[:, h * HALF : (h + 1) * HALF] = jnp.dot(
            spread_ref[...], fetched[h].reshape(PLACES, HALF), preferred_element_type=F32
        ).astype(BF16)

    stores = []
    for b in range(NB):
        ref = weights.at[b, :, 1 - here.core]
        remote(ref, ref, core_send.at[b], core_recv.at[b], here.partner()).wait_recv()
        dst = key_ref if b < NB // 2 else value_ref
        stores.append(
            pltpu.make_async_copy(
                weights.at[b], dst.at[:, :, :, pl.ds((b % (NB // 2)) * CB, CB)], store_sem.at[b]
            )
        )
        stores[-1].start()
    for b in range(NB):
        to_partner(b).wait_send()
    for ring in tables + pieces:
        ring.drain()
    for i in range(1, Z):
        for cross in crosses:
            cross.drain(zeds[i], i)
    mates_sent(here, req_out, req_send)
    for h in range(2):
        mates_sent(here, reply.at[h], rep_send.at[h])
    for store in stores:
        store.wait()


def gather_call(owner, local, expand, table, w_key, w_value):
    vmem = pl.BlockSpec(memory_space=pltpu.VMEM)
    any_ = pl.BlockSpec(memory_space=pl.ANY)
    dma = pltpu.SemaphoreType.DMA
    return pl.pallas_call(
        gather_kernel,
        out_shape=(
            jax.ShapeDtypeStruct((TOK, E), BF16),
            jax.ShapeDtypeStruct((TOK, PLACES), BF16),
            jax.ShapeDtypeStruct((PLACES, Z * TROWS), BF16),
            jax.ShapeDtypeStruct((Z, 2, WROWS, D), BF16),
            jax.ShapeDtypeStruct((Z, 2, WROWS, D), BF16),
        ),
        in_specs=[vmem, vmem, vmem, vmem, any_, any_],
        out_specs=(vmem, vmem, vmem, any_, any_),
        scratch_shapes=[
            pltpu.VMEM((NB, Z, 2, WROWS, CB), BF16),
            pltpu.VMEM((2, Z, TROWS, HALF), BF16),
            pltpu.VMEM((PLANE, 1, 128), F32),
            pltpu.VMEM((PLANE, 1, 128), F32),
            pltpu.VMEM((2, PLANE, MSG, HALF), BF16),
            pltpu.VMEM((2, PLANE, MSG, HALF), BF16),
            dma((NB,)), dma((NB,)), dma, dma, dma((2,)), dma((2,)),
            dma((2, 2, 4)), dma((2, 2, 4)), dma((4, 2, 4)), dma((4, 2, 4)),
            dma((2, 4, Z)), dma((2, 4, Z)), dma((NB,)), dma((NB,)),
        ],
        compiler_params=pltpu.CompilerParams(
            collective_id=0, has_side_effects=True, vmem_limit_bytes=48 * 1024 * 1024
        ),
        name="gather_rows_and_weights",
    )(owner, local, expand, table, w_key, w_value)


def adamw(current, moment, second, gradient):
    moment_new = BETA_ONE * moment + (1.0 - BETA_ONE) * gradient
    second_new = BETA_TWO * second + (1.0 - BETA_TWO) * gradient * gradient
    first_hat = moment_new / (1.0 - BETA_ONE**STEP_COUNT)
    second_hat = second_new / (1.0 - BETA_TWO**STEP_COUNT)
    updated = current - LEARN_RATE * (first_hat / (jnp.sqrt(second_hat) + ADAM_EPS) + DECAY_RATE * current)
    return updated, moment_new, second_new


def transposed_dot(left, right):
    return lax.dot_general(left, right, (((0,), (0,)), ((), ())), preferred_element_type=F32)


def return_kernel(
    grad_ref, spread_ref, serve_ref, table_ref, m_ref, v_ref,
    out_table, out_m, out_v,
    slots, arrived, partial, give, take,
    slot_send, slot_recv, ring_send, ring_recv,
):
    here = Here()
    greeted = greet(here)
    for h in range(2):
        lanes = slice(h * HALF, (h + 1) * HALF)
        rows = transposed_dot(spread_ref[...], grad_ref[:, lanes])
        slots[h] = rows.astype(BF16).reshape(PLANE, MSG, HALF)
        arrived[h, here.plane] = slots[h, here.plane]
    greeted()
    for h in range(2):
        send_mates(here, slots.at[h], arrived.at[h], slot_send.at[h], slot_recv.at[h])

    def hop(h, way, step):
        sign = 1 if way == 0 else -1
        return remote(
            give.at[h, way, step - 1], take.at[h, way, step - 1],
            ring_send.at[h, way, step - 1], ring_recv.at[h, way, step - 1], here.at_z(sign),
        )

    def length(h, way):
        return Z // 2 if way == h else Z // 2 - 1

    def advance(h, step):
        for way in range(2):
            last = length(h, way)
            if step > last:
                continue
            sign = 1 if way == 0 else -1
            mine = partial[h, here.zed(sign * (last - step + 1))]
            if step > 1:
                hop(h, way, step - 1).wait_recv()
                mine = mine + take[h, way, step - 2].astype(F32)
            give[h, way, step - 1] = mine.astype(BF16)
            hop(h, way, step).start()

    for h in range(2):
        mates_arrived(here, arrived.at[h], slot_recv.at[h])
        rows = transposed_dot(serve_ref[...], arrived[h].reshape(PLACES, HALF))
        partial[h] = rows.reshape(Z, TROWS, HALF)
        advance(h, 1)
    for step in (2, 3, 4):
        for h in range(2):
            advance(h, step)
    for h in range(2):
        lanes = slice(h * HALF, (h + 1) * HALF)
        total = partial[h, here.z]
        for way in range(2):
            last = length(h, way)
            hop(h, way, last).wait_recv()
            total = total + take[h, way, last - 1].astype(F32)
        new_t, new_m, new_v = adamw(table_ref[:, lanes], m_ref[:, lanes], v_ref[:, lanes], total[:R_DEV])
        out_table[:, lanes] = new_t
        out_m[:, lanes] = new_m
        out_v[:, lanes] = new_v
    for h in range(2):
        mates_sent(here, slots.at[h], slot_send.at[h])
        for way in range(2):
            for step in range(1, length(h, way) + 1):
                hop(h, way, step).wait_send()


def return_call(memory_grad, spread, serve, table, adam_m, adam_v):
    vmem = pl.BlockSpec(memory_space=pltpu.VMEM)
    dma = pltpu.SemaphoreType.DMA
    return pl.pallas_call(
        return_kernel,
        out_shape=tuple(jax.ShapeDtypeStruct((R_DEV, E), F32) for _ in range(3)),
        in_specs=[vmem] * 6,
        out_specs=(vmem,) * 3,
        scratch_shapes=[
            pltpu.VMEM((2, PLANE, MSG, HALF), BF16),
            pltpu.VMEM((2, PLANE, MSG, HALF), BF16),
            pltpu.VMEM((2, Z, TROWS, HALF), F32),
            pltpu.VMEM((2, 2, 4, TROWS, HALF), BF16),
            pltpu.VMEM((2, 2, 4, TROWS, HALF), BF16),
            dma((2,)), dma((2,)), dma((2, 2, 4)), dma((2, 2, 4)),
        ],
        compiler_params=pltpu.CompilerParams(
            collective_id=1, has_side_effects=True, vmem_limit_bytes=32 * 1024 * 1024
        ),
        name="return_row_gradients",
    )(memory_grad, spread, serve, table, adam_m, adam_v)


def from_behind(value, axis, steps):
    count = lax.axis_size(axis)
    first, last = (max(0, -steps), min(count, count - steps))
    return lax.ppermute(value, axis, [(source, source + steps) for source in range(first, last)])


def rms_scale(values):
    return lax.rsqrt(jnp.mean(values * values, axis=-1, keepdims=True) + NORM_EPS)


def doc_index(positions, lengths):
    k = jnp.arange(lengths.shape[0], dtype=jnp.int32)
    doc_ends = jnp.sum(jnp.where(k[None, :] <= k[:, None], lengths[None, :], 0), axis=1)
    return jnp.sum((positions[:, None] >= doc_ends[None, :-1]).astype(jnp.int32), axis=1)


def contract_last(left, right):
    return lax.dot_general(
        left, right, (((1,), (1,)), ((), ())), preferred_element_type=jnp.float32
    )


def on_device(
    hidden, grad_out, w_key, w_value, depthwise_weight, table, adam_m, adam_v,
    row_owner, row_local, expand_index, doc_lengths,
):
    tok_count = hidden.shape[1]
    model_width = hidden.shape[2]
    kernel_taps = depthwise_weight.shape[0]
    border_rows = DILATION_STEP * (kernel_taps - 1)
    root_width = jnp.sqrt(jnp.float32(model_width))
    memory, spread, serve, key_full, value_full = gather_call(
        row_owner[0], row_local, expand_index[0], table, w_key, w_value
    )
    key_full = key_full.reshape(E, D)
    value_full = value_full.reshape(E, D)
    key = jnp.dot(memory, key_full, preferred_element_type=jnp.float32)
    value = jnp.dot(memory, value_full, preferred_element_type=jnp.float32)
    key_scale = rms_scale(key)
    key_norm = key * key_scale
    hidden_f = hidden[0].astype(jnp.float32)
    hidden_norm = hidden_f * rms_scale(hidden_f)
    gate = jax.nn.sigmoid(jnp.sum(hidden_norm * key_norm, axis=-1, keepdims=True) / root_width)
    gated = (gate * value).astype(jnp.bfloat16)
    gated_f = gated.astype(jnp.float32)
    gated_scale = rms_scale(gated_f)
    gated_normalized = gated_f * gated_scale
    lengths = doc_lengths[0]
    first_pos = lax.axis_index("col") * tok_count
    earlier = from_behind(gated[tok_count - border_rows :], "col", 1)
    extended = jnp.concatenate([earlier, gated], axis=0).astype(jnp.float32)
    extended_norm = extended * rms_scale(extended)
    pos_before = first_pos - border_rows + jnp.arange(tok_count + border_rows, dtype=jnp.int32)
    doc_before = doc_index(pos_before, lengths)
    doc_here = doc_before[border_rows:]
    convolved_rows = jnp.zeros((tok_count, model_width), jnp.float32)
    for kernel_tap_index in range(kernel_taps):
        shift_amount = kernel_tap_index * DILATION_STEP
        source_pos = pos_before[border_rows - shift_amount : border_rows - shift_amount + tok_count]
        source_doc = doc_before[border_rows - shift_amount : border_rows - shift_amount + tok_count]
        same_doc = ((source_pos >= 0) & (source_doc == doc_here)).astype(jnp.float32)[:, None]
        convolved_rows = (
            convolved_rows
            + depthwise_weight[kernel_tap_index]
            * extended_norm[border_rows - shift_amount : border_rows - shift_amount + tok_count]
            * same_doc
        )
    memory_out = (jax.nn.silu(convolved_rows) + gated_f).astype(jnp.bfloat16)
    grad_f = grad_out[0].astype(jnp.float32)
    sig = jax.nn.sigmoid(convolved_rows)
    convolution_gradient = grad_f * sig * (1.0 + convolved_rows * (1.0 - sig))
    next_rows = from_behind(
        convolution_gradient[:border_rows].astype(jnp.bfloat16), "col", -1
    ).astype(jnp.float32)
    grad_ext = jnp.concatenate([convolution_gradient, next_rows], axis=0)
    pos_after = first_pos + jnp.arange(tok_count + border_rows, dtype=jnp.int32)
    doc_after = doc_index(pos_after, lengths)
    normalized_gradient = jnp.zeros((tok_count, model_width), jnp.float32)
    for kernel_tap_index in range(kernel_taps):
        shift_amount = kernel_tap_index * DILATION_STEP
        same_doc = (
            doc_after[shift_amount : shift_amount + tok_count] == doc_after[:tok_count]
        ).astype(jnp.float32)[:, None]
        normalized_gradient = normalized_gradient + depthwise_weight[kernel_tap_index] * (
            grad_ext[shift_amount : shift_amount + tok_count] * same_doc
        )
    gated_grad = grad_f + gated_scale * (
        normalized_gradient
        - gated_normalized
        * jnp.mean(gated_normalized * normalized_gradient, axis=-1, keepdims=True)
    )
    value_grad = gated_grad * gate
    score_grad = gate * (1.0 - gate) * jnp.sum(gated_grad * value, axis=-1, keepdims=True)
    target = score_grad * hidden_norm / root_width
    key_grad = key_scale * (target - key_norm * jnp.mean(key_norm * target, axis=-1, keepdims=True))
    key_grad16 = key_grad.astype(jnp.bfloat16)
    value_grad16 = value_grad.astype(jnp.bfloat16)
    memory_grad = (
        contract_last(key_grad16, key_full) + contract_last(value_grad16, value_full)
    ).astype(jnp.bfloat16)
    new_table, new_moment, new_second = return_call(memory_grad, spread, serve, table, adam_m, adam_v)
    return (memory_out[None], new_table, new_moment, new_second)


def solution(mesh):
    placed = (
        P("row", "col", None),
        P("row", "col", None),
        P("row", None),
        P("row", None),
        P(),
        P(("row", "col"), None),
        P(("row", "col"), None),
        P(("row", "col"), None),
        P("row", "col", None),
        P("row", "col"),
        P("row", "col", None),
        P("row", None),
    )
    return jax.shard_map(
        on_device,
        mesh=mesh,
        in_specs=placed,
        out_specs=(
            P("row", "col", None),
            P(("row", "col"), None),
            P(("row", "col"), None),
            P(("row", "col"), None),
        ),
        check_vma=False,
    )
```

time: 246 us -> 158 us (0.64)
  the two profiles are of different devices: /device:TPU:1 before, /device:TPU:34 now
where the time goes in v1:
time: 158 us; the launch traced here: 157 us
  Pallas kernels  115 us (73%)
  matrix products  10.6 us (7%)
  waiting for transfers between devices  9.89 us (6%)
  local copies, waits for them, and re-layouts  7.95 us (5%)
  other arithmetic  7.4 us (5%)
  starting transfers between devices  5.2 us (3%)
    pallas_call x1, Pallas kernels, gather_call(): pl.pallas_call(gather_kernel, out_shape=(jax.ShapeDtypeStruct((TOK, E), B...  76 us
    pallas_call x1, Pallas kernels, return_call(): pl.pallas_call(return_kernel, out_shape=tuple((jax.ShapeDtypeStruct((R_DE...  39.2 us
    ppermute x2, waiting for transfers between devices, from_behind(): lax.ppermute(value, axis, [(source, source + steps) for source in range(f...  9.89 us
    unnamed x40, local copies, waits for them, and re-layouts  7.03 us
    ppermute x2, starting transfers between devices, from_behind(): lax.ppermute(value, axis, [(source, source + steps) for source in range(f...  5.2 us
    dot_general x2, matrix products, contract_last(): lax.dot_general(left, right, (((1,), (1,)), ((), ())), preferred_element_...  4.36 us
    dot_general x1, matrix products, on_device(): key = jnp.dot(memory, key_full, preferred_element_type=jnp.float32)  4.13 us
  transfers between devices with their start and end apart: 2, of which 2 were waited for; matrix products, arithmetic and copies ran while one was open for 0% of the time, Pallas kernels for 0%

profile of v1, /device:TPU:34, one launch (start us, length us, event | category | flops | bytes accessed | tf_op | source)
XLA Modules:
  0.0 157.2 jit_solution(11914353498033706517)
XLA Ops:
  0.6 0.8 copy.20.owner_ref
  1.4 0.8 copy.19
  2.2 1.3 fusion.25
  3.5 0.9 copy-done
  4.4 1.0 copy-done.2
  5.4 1.0 copy-done.3
  6.4 0.7 copy-done.6
  7.1 76.0 %gather_rows_and_weights.1 = (bf16[128,1280]{1,0:T(8,128)(2,1)S(1)}, bf16[128,512]{1,0:T(8,128)(2,1)S(1)}, bf16[512,384]{1,0:T(8,128)(2,1)S(1)}, bf16[8,2,80,256...) custom-call(s32[144,1]{1,0:T(8,128)S(1)} %copy.20.owner_ref, s32[1,144]{1,0:T(1,128)S(1)} %copy-done.6, s32[128,2]{1,0:T(8,128)S(1)} %bitcast.32, ...), custom_call_target="tpu_custom_call" | custom-call | tf_op jit(solution)/shard_map/gather_rows_and_weights/pallas_call | solution.py:358
  83.2 4.1 %multiply_reduce_fusion.1 = (f32[128]{0:T(128)S(1)}, f32[128,2560]{1,0:T(8,128)S(1)}) fusion(bf16[128,1280]{1,0:T(8,128)(2,1)S(1)} %get-tuple-element.12, bf16[1280,2560]{1,0:T(8,128)(2,1)} %bitcast.39), kind=kOutput, calls=%fused_computation.61 | convolution fusion | flops 839516032 | bytes 8192512 | tf_op jit(solution)/shard_map/dot_general | solution.py:525
  88.1 2.1 %fusion.28 = (f32[128]{0:T(128)S(1)}, bf16[128,2560]{1,0:T(8,128)(2,1)S(1)}, f32[128,2560]{1,0:T(8,128)}) fusion(f32[128]{0:T(128)S(1)} %add_divide_fusion.1, bf16[128,1280]{1,0:T(8,128)(2,1)S(1)} %get-tuple-element.12, bf16[1280,2560]{1,0:T(8,128)(2,1)S(1)} %bitcast.35), kind=kOutput, calls=%fused_computation.42 | convolution fusion | flops 840499072 | bytes 8848384 | tf_op jit(solution)/shard_map/dot_general | solution.py:526
  90.3 1.9 %collective-permute-start = (bf16[9,2560]{1,0:T(8,128)(2,1)S(1)}, bf16[9,2560]{1,0:T(8,128)(2,1)S(1)}, u32[]{:S(2)}, u32[]{:S(2)}) collective-permute-start(bf16[9,2560]{1,0:T(8,128)(2,1)S(1)} %slice.115), channel_id=1, source_target_pairs={{0,1},{1,2},{2,3},{3,4},{4,5},{5,6},{6,7},{7,8},{8,9},{9,10},{10,1... | collective-permute-start | bytes 138248 | tf_op jit(solution)/shard_map/ppermute | solution.py:492
  92.7 6.0 %collective-permute-done = bf16[9,2560]{1,0:T(8,128)(2,1)S(1)} collective-permute-done((bf16[9,2560]{1,0:T(8,128)(2,1)S(1)}, bf16[9,2560]{1,0:T(8,128)(2,1)S(1)}, u32[]{:S(2)}, u32[]{:S(2)}) %collective-permute-start) | collective-permute-done | bytes 46112 | tf_op jit(solution)/shard_map/ppermute | solution.py:492
  99.4 1.2 fusion.26
  100.7 3.3 %collective-permute-start.1 = (bf16[9,2560]{1,0:T(8,128)(2,1)S(1)}, bf16[9,2560]{1,0:T(8,128)(2,1)S(1)}, u32[]{:S(2)}, u32[]{:S(2)}) collective-permute-start(bf16[9,2560]{1,0:T(8,128)(2,1)S(1)} %slice.198), channel_id=1, source_target_pairs={{1,0},{2,1},{3,2},{4,3},{5,4},{6,5},{7,6},{8,7},{9,8},{10,9},{11,1... | collective-permute-start | bytes 138248 | tf_op jit(solution)/shard_map/ppermute | solution.py:492
  104.0 3.9 %collective-permute-done.1 = bf16[9,2560]{1,0:T(8,128)(2,1)S(1)} collective-permute-done((bf16[9,2560]{1,0:T(8,128)(2,1)S(1)}, bf16[9,2560]{1,0:T(8,128)(2,1)S(1)}, u32[]{:S(2)}, u32[]{:S(2)}) %collective-permute-start.1) | collective-permute-done | bytes 46112 | tf_op jit(solution)/shard_map/ppermute | solution.py:492
  107.9 1.2 fusion.15
  109.2 1.8 %multiply_reduce_fusion = (f32[128]{0:T(128)S(1)}, bf16[1,128,2560]{2,1,0:T(8,128)(2,1)}) fusion(f32[128,2560]{1,0:T(8,128)S(1)} %copy-done.9, f32[128,2560]{1,0:T(8,128)S(1)} %get-tuple-element.27, f32[128]{0:T(128)S(1)} %broadcast_multiply_fusion.1, bf16[128,2560]{1,0:T(8,128)(2,1)S(1)} %get-tuple-element.29, f32[128]{0:T(128)S(1)} %add_rsqrt_fusion.1, ...), kind=kLoop, calls=%fused_computation.58 | loop fusion | flops 4915072 | bytes 5899776 | tf_op jit(solution)/shard_map/reduce_sum | solution.py:581
  111.0 0.5 fusion.22
  111.5 2.2 %fusion.38 = f32[128,1280]{1,0:T(8,128)S(1)} fusion(bf16[1280,2560]{1,0:T(8,128)(2,1)S(1)} %bitcast.42, f32[128,2560]{1,0:T(8,128)S(1)} %get-tuple-element.42, bf16[1,128,2560]{2,1,0:T(8,128)(2,1)S(1)} %copy-done.7, f32[128]{0:T(128)S(1)} %broadcast_multiply_fusion, f32[128]{0:T(128)S(1)} %fusion.48, f32[128]{0:T(128)S(1)} %get-tuple-element.44, ...), kind=kOutput, calls=%fused_computation.63 | convolution fusion | flops 841809920 | bytes 9177088 | tf_op jit(solution)/shard_map/dot_general | solution.py:506
  113.7 2.2 %fusion.grad_ref = bf16[128,1280]{1,0:T(8,128)(2,1)S(1)} fusion(f32[128,1280]{1,0:T(8,128)S(1)} %fusion.38, bf16[1280,2560]{1,0:T(8,128)(2,1)S(1)} %bitcast.38, f32[128]{0:T(128)S(1)} %add_divide_fusion.1, f32[128,2560]{1,0:T(8,128)S(1)} %get-tuple-element.27, bf16[128,2560]{1,0:T(8,128)(2,1)S(1)} %get-tuple-element.29, ...), kind=kOutput, calls=%fused_computation.1 | convolution fusion | flops 842137600 | bytes 10159616 | tf_op jit(solution)/shard_map/dot_general | solution.py:506
  115.9 39.2 %return_row_gradients.1 = (f32[40,1280]{1,0:T(8,128)S(1)}, f32[40,1280]{1,0:T(8,128)S(1)}, f32[40,1280]{1,0:T(8,128)S(1)}) custom-call(bf16[128,1280]{1,0:T(8,128)(2,1)S(1)} %fusion.grad_ref, bf16[128,512]{1,0:T(8,128)(2,1)S(1)} %get-tuple-element.15.spread_ref, bf16[512,384]{1,0:T(8,128)(2,1)S(1)} %get-tuple-element.16.serve_ref, f32[40,1280]{1,0:T(8,128)S(1)} %copy-done.1, ...), custom_call_target="tpu_custom_call" | custom-call | tf_op jit(solution)/shard_map/return_row_gradients/pallas_call | solution.py:469
  155.2 0.7 copy.24
  155.8 0.7 copy.25
  156.5 0.7 copy.26
  (54 shorter events, 2.2 us)
Async XLA Ops:
  3.5 0.9 copy-start
  4.4 1.0 copy-start.2
  5.4 1.0 copy-start.3
  6.4 0.7 copy-start.6
  83.1 4.6 %slice-start = ((s8[6553600]{0:T(1024)(128)(4,1)}), s8[4194304]{0:T(1024)(128)(4,1)S(1)}, s32[]{:S(2)}) async-start(s8[6553600]{0:T(1024)(128)(4,1)} %bitcast.33), calls=%async_computation | async-start | bytes 8388608
  83.1 4.2 %copy-start.7 = (bf16[1,128,2560]{2,1,0:T(8,128)(2,1)S(1)}, bf16[1,128,2560]{2,1,0:T(8,128)(2,1)}, u32[]{:S(2)}) copy-start(bf16[1,128,2560]{2,1,0:T(8,128)(2,1)} %param.12) | copy-start | bytes 1966084
  83.2 5.0 %slice-start.1 = ((s8[6553600]{0:T(1024)(128)(4,1)}), s8[2359296]{0:T(1024)(128)(4,1)S(1)}, s32[]{:S(2)}) async-start(s8[6553600]{0:T(1024)(128)(4,1)} %bitcast.33), calls=%async_computation.1 | async-start | bytes 4718592
  88.1 4.1 %copy-start.11 = (s32[1,8]{1,0:T(1,128)S(1)}, s32[1,8]{1,0:T(1,128)}, u32[]{:S(2)}) copy-start(s32[1,8]{1,0:T(1,128)} %param.23) | copy-start | bytes 100
  88.1 4.5 %copy-start.10 = (f32[4,2560]{1,0:T(4,128)S(1)}, f32[4,2560]{1,0:T(4,128)}, u32[]{:S(2)}) copy-start(f32[4,2560]{1,0:T(4,128)} %param.16) | copy-start | bytes 122884
  90.3 8.4 %collective-permute-start = (bf16[9,2560]{1,0:T(8,128)(2,1)S(1)}, bf16[9,2560]{1,0:T(8,128)(2,1)S(1)}, u32[]{:S(2)}, u32[]{:S(2)}) collective-permute-start(bf16[9,2560]{1,0:T(8,128)(2,1)S(1)} %slice.115), channel_id=1, source_target_pairs={{0,1},{1,2},{2,3},{3,4},{4,5},{5,6},{6,7},{7,8},{8,9},{9,10},{10,1... | collective-permute-start | bytes 138248 | tf_op jit(solution)/shard_map/ppermute | solution.py:492
  92.7 6.7 %copy-start.8 = (bf16[1,128,2560]{2,1,0:T(8,128)(2,1)S(1)}, bf16[1,128,2560]{2,1,0:T(8,128)(2,1)}, u32[]{:S(2)}) copy-start(bf16[1,128,2560]{2,1,0:T(8,128)(2,1)} %param.13) | copy-start | bytes 1966084
  99.4 12.1 %slice-start.4 = ((s8[6553600]{0:T(1024)(128)(4,1)}), s8[4194304]{0:T(1024)(128)(4,1)S(1)}, s32[]{:S(2)}) async-start(s8[6553600]{0:T(1024)(128)(4,1)} %bitcast.40), calls=%async_computation.4 | async-start | bytes 8388608
  100.7 7.2 %collective-permute-start.1 = (bf16[9,2560]{1,0:T(8,128)(2,1)S(1)}, bf16[9,2560]{1,0:T(8,128)(2,1)S(1)}, u32[]{:S(2)}, u32[]{:S(2)}) collective-permute-start(bf16[9,2560]{1,0:T(8,128)(2,1)S(1)} %slice.198), channel_id=1, source_target_pairs={{1,0},{2,1},{3,2},{4,3},{5,4},{6,5},{7,6},{8,7},{9,8},{10,9},{11,1... | collective-permute-start | bytes 138248 | tf_op jit(solution)/shard_map/ppermute | solution.py:492
  107.8 1.3 copy-start.9
  107.9 3.6 %slice-start.5 = ((s8[6553600]{0:T(1024)(128)(4,1)}), s8[2359296]{0:T(1024)(128)(4,1)S(1)}, s32[]{:S(2)}) async-start(s8[6553600]{0:T(1024)(128)(4,1)} %bitcast.40), calls=%async_computation.5 | async-start | bytes 4718592
  109.2 4.5 %slice-start.2 = ((s8[6553600]{0:T(1024)(128)(4,1)}), s8[4194304]{0:T(1024)(128)(4,1)S(1)}, s32[]{:S(2)}) async-start(s8[6553600]{0:T(1024)(128)(4,1)} %bitcast.36), calls=%async_computation.2 | async-start | bytes 8388608
  111.5 2.2 %slice-start.3 = ((s8[6553600]{0:T(1024)(128)(4,1)}), s8[2359296]{0:T(1024)(128)(4,1)S(1)}, s32[]{:S(2)}) async-start(s8[6553600]{0:T(1024)(128)(4,1)} %bitcast.36), calls=%async_computation.3 | async-start | bytes 4718592
  113.7 2.2 %copy-start.1 = (f32[40,1280]{1,0:T(8,128)S(1)}, f32[40,1280]{1,0:T(8,128)}, u32[]{:S(2)}) copy-start(f32[40,1280]{1,0:T(8,128)} %table_ref.3) | copy-start | bytes 614404
  113.7 2.2 %copy-start.4 = (f32[40,1280]{1,0:T(8,128)S(1)}, f32[40,1280]{1,0:T(8,128)}, u32[]{:S(2)}) copy-start(f32[40,1280]{1,0:T(8,128)} %m_ref.1) | copy-start | bytes 614404
  113.7 2.2 %copy-start.5 = (f32[40,1280]{1,0:T(8,128)S(1)}, f32[40,1280]{1,0:T(8,128)}, u32[]{:S(2)}) copy-start(f32[40,1280]{1,0:T(8,128)} %v_ref.1) | copy-start | bytes 614404

commit v2 on v1

v2 whole, which is shorter than its diff:
```python
import jax
import jax.numpy as jnp
from jax import lax
from jax.experimental import pallas as pl
from jax.experimental.pallas import tpu as pltpu
from jax.sharding import PartitionSpec as P

DILATION_STEP = 3
NORM_EPS = 1e-06
BETA_ONE = 0.9
BETA_TWO = 0.95
ADAM_EPS = 1e-08
LEARN_RATE = 0.01
DECAY_RATE = 0.1
STEP_COUNT = 10.0

Z, X, Y = 8, 4, 4
PLANE = 2 * X * Y
D, E = 2560, 1280
TOK, U, R_DEV = 128, 144, 40
CW = 256
NC = E // CW
TROWS = 48
MSG = 2 * Z
PLACES = PLANE * MSG
CB = 512
NB = 2 * D // CB
WROWS = 80
TILE = 16
PAD = 16
TAPS = 4

MESH = pl.DeviceIdType.MESH
F32, BF16, I32 = jnp.float32, jnp.bfloat16, jnp.int32


class Here:
    def __init__(self):
        self.row = lax.axis_index("row")
        self.col = lax.axis_index("col")
        self.z = self.row // 2
        self.core = self.row % 2
        self.x = self.col // Y
        self.y = self.col % Y
        self.plane = self.core * (X * Y) + self.col

    def mate(self, i):
        q = lax.rem(self.plane + i, PLANE)
        return q, (self.z * 2 + q // (X * Y), q % (X * Y))

    def zed(self, step):
        return lax.rem(self.z + step + Z, Z)

    def at_z(self, step):
        return (self.zed(step) * 2 + self.core, self.col)

    def exx(self, step):
        return lax.rem(self.x + step + X, X)

    def wye(self, step):
        return lax.rem(self.y + step + Y, Y)

    def at_x(self, step):
        return (self.row, self.exx(step) * Y + self.y)

    def at_y(self, step):
        return (self.row, self.x * Y + self.wye(step))

    def partner(self):
        return (self.z * 2 + 1 - self.core, self.col)


def remote(src, dst, send, recv, device):
    return pltpu.make_async_remote_copy(
        src_ref=src, dst_ref=dst, send_sem=send, recv_sem=recv, device_id=device, device_id_type=MESH
    )


def greet(here):
    barrier = pltpu.get_barrier_semaphore()

    def one(i, carry):
        _, device = here.mate(i)
        pl.semaphore_signal(barrier, inc=1, device_id=device, device_id_type=MESH)
        return carry

    lax.fori_loop(1, PLANE, one, 0)
    for step in (1, -1):
        pl.semaphore_signal(barrier, inc=1, device_id=here.at_z(step), device_id_type=MESH)
    return lambda: pl.semaphore_wait(barrier, PLANE + 1)


def iota(shape, dim):
    return lax.broadcasted_iota(I32, shape, dim)


def one_hot(mask):
    return jnp.where(mask, 1.0, 0.0).astype(BF16)


def nn(left, right):
    return jnp.dot(left, right, preferred_element_type=F32)


def tn(left, right):
    return lax.dot_general(left, right, (((0,), (0,)), ((), ())), preferred_element_type=F32)


def nt(left, right):
    return lax.dot_general(left, right, (((1,), (1,)), ((), ())), preferred_element_type=F32)


def column_of(row, size):
    eye = iota((size, size), 0) == iota((size, size), 1)
    return jnp.sum(jnp.where(eye, row, 0), axis=1, keepdims=True)


def plan_slots(owner_ref, local_ref, expand_ref, spread, spread_t, req_out):
    owner_r = owner_ref[...]
    owner_c = column_of(owner_r, U)
    local_c = column_of(local_ref[...], U)
    same = owner_c == owner_r
    earlier_c = same & (iota((U, U), 1) < iota((U, U), 0))
    earlier_r = same & (iota((U, U), 0) < iota((U, U), 1))
    k_c = (owner_c >> 5) * 2 + jnp.sum(jnp.where(earlier_c, 1, 0), axis=1, keepdims=True)
    k_r = (owner_r >> 5) * 2 + jnp.sum(jnp.where(earlier_r, 1, 0), axis=0, keepdims=True)
    mates = one_hot((owner_r & 31) == iota((PLANE, U), 0))
    wanted = jnp.where(k_c == iota((U, 128), 1), local_c + 1, 0).astype(F32).astype(BF16)
    request = nn(mates, wanted)
    for q in range(PLANE):
        req_out[q] = request[q : q + 1, :]
    expand = expand_ref[...]
    reads = jnp.zeros((U, TOK), F32)
    for lookup in range(2):
        reads = reads + jnp.where(expand[lookup : lookup + 1, :] == iota((U, TOK), 0), 1.0, 0.0)
    reads = reads.astype(BF16)
    places = one_hot((owner_c & 31) * MSG + k_c == iota((U, PLACES), 1))
    places_t = one_hot((owner_r & 31) * MSG + k_r == iota((PLACES, U), 0))
    spread[...] = tn(reads, places).astype(BF16)
    spread_t[...] = nn(places_t, reads).astype(BF16)


def plan_serve(req_in, serve, serve_t):
    asked = req_in[:, 0, :].astype(BF16)
    wide = nn(one_hot(iota((PLACES, PLANE), 0) // MSG == iota((PLACES, PLANE), 1)), asked)
    k = iota((PLACES, 128), 0) % MSG
    value = jnp.sum(jnp.where(k == iota((PLACES, 128), 1), wide, 0.0), axis=1, keepdims=True)
    zed = (iota((PLACES, 1), 0) % MSG) // 2
    target = jnp.where(value > 0.5, zed * TROWS + value.astype(I32) - 1, -1)
    serve[...] = one_hot(target == iota((PLACES, Z * TROWS), 1))
    tall = tn(asked, one_hot(iota((PLANE, PLACES), 1) // MSG == iota((PLANE, PLACES), 0)))
    k = iota((128, PLACES), 1) % MSG
    value = jnp.sum(jnp.where(k == iota((128, PLACES), 0), tall, 0.0), axis=0, keepdims=True)
    zed = (iota((1, PLACES), 1) % MSG) // 2
    target = jnp.where(value > 0.5, zed * TROWS + value.astype(I32) - 1, -1)
    serve_t[...] = one_hot(target == iota((Z * TROWS, PLACES), 0))


def plan_docs(here, lengths_ref, docs):
    n = lengths_ref.shape[1]
    length_c = column_of(lengths_ref[...], n)
    ends = jnp.sum(jnp.where(iota((n, n), 0) <= iota((n, n), 1), length_c, 0), axis=0, keepdims=True)
    rows = docs.shape[0]
    position = here.col * TOK - PAD + iota((rows, 1), 0)
    passed = (position >= ends) & (iota((rows, n), 1) < n - 1)
    doc = jnp.sum(jnp.where(passed, 1.0, 0.0), axis=1, keepdims=True)
    doc = jnp.where(position < 0, -1.0, jnp.where(position >= 16 * TOK, -2.0, doc))
    docs[...] = jnp.broadcast_to(doc, (rows, 128))


def send_mates(here, src, dst, send, recv):
    def one(i, carry):
        q, device = here.mate(i)
        remote(src.at[q], dst.at[here.plane], send, recv, device).start()
        return carry

    lax.fori_loop(1, PLANE, one, 0)


def mates_arrived(here, dst, recv):
    ref = dst.at[pl.ds(0, PLANE - 1)]
    pltpu.make_async_copy(ref, ref, recv).wait()


def mates_sent(here, src, send):
    ref = src.at[pl.ds(0, PLANE - 1)]
    pltpu.make_async_copy(ref, ref, send).wait()


class Ring:
    def __init__(self, here, block, send, recv, far):
        self.here, self.block, self.send, self.recv, self.far = here, block, send, recv, far

    def copy(self, way, step):
        sign = 1 if way == 0 else -1
        ref = self.block(self.here.zed(-sign * (step - 1)))
        return remote(ref, ref, self.send.at[way, step - 1], self.recv.at[way, step - 1], self.here.at_z(sign))

    def steps(self, way):
        return Z // 2 if way == self.far else Z // 2 - 1

    def start(self, step):
        for way in range(2):
            if step <= self.steps(way):
                self.copy(way, step).start()

    def arrived(self, step):
        got = []
        for way in range(2):
            if step <= self.steps(way):
                sign = 1 if way == 0 else -1
                ref = self.block(self.here.zed(-sign * step))
                remote(ref, ref, self.send.at[way, step - 1], self.recv.at[way, step - 1], self.here.at_z(-sign)).wait_recv()
                got.append(-sign * step)
        return got

    def drain(self):
        for way in range(2):
            for step in range(1, self.steps(way) + 1):
                self.copy(way, step).wait_send()


class Cross:
    def __init__(self, here, axis, weights, base, send, recv):
        self.here, self.weights, self.base, self.send, self.recv = here, weights, base, send, recv
        self.at = here.at_x if axis == "x" else here.at_y
        self.place = here.exx if axis == "x" else here.wye

    def copy(self, way, zz, i):
        sign = 1 if way % 2 == 0 else -1
        if way < 2:
            ref = self.weights.at[self.base + self.place(0), zz, self.here.core]
        else:
            ref = self.weights.at[self.base + self.place(-sign), zz, self.here.core, :, pl.ds((way - 2) * (CB // 2), CB // 2)]
        return remote(ref, ref, self.send.at[way, i], self.recv.at[way, i], self.at(sign))

    def got(self, way, zz, i):
        sign = 1 if way % 2 == 0 else -1
        if way < 2:
            ref = self.weights.at[self.base + self.place(-sign), zz, self.here.core]
        else:
            ref = self.weights.at[
                self.base + self.place(-2 * sign), zz, self.here.core, :, pl.ds((way - 2) * (CB // 2), CB // 2)
            ]
        return remote(ref, ref, self.send.at[way, i], self.recv.at[way, i], self.at(-sign))

    def start(self, zz, i):
        for way in (0, 1):
            self.copy(way, zz, i).start()

    def relay(self, zz, i):
        for way in (0, 1):
            self.got(way, zz, i).wait_recv()
            self.copy(way + 2, zz, i).start()

    def finish(self, zz, i):
        for way in (2, 3):
            self.got(way, zz, i).wait_recv()

    def drain(self, zz, i):
        for way in range(4):
            self.copy(way, zz, i).wait_send()


def lanes(b):
    return slice((b % (NB // 2)) * CB, (b % (NB // 2) + 1) * CB)


def row_tile(t):
    return pl.ds(pl.multiple_of(t * TILE, TILE), TILE)


def mean_scale(total):
    return lax.rsqrt(total / D + NORM_EPS)


BLOCKS = range(NB // 2)
STATS = ("key_scale", "hidden_scale", "score", "gate", "gated_scale")


def keep(stats, name, rows, value):
    stats[STATS.index(name), rows, :] = jnp.broadcast_to(value, (TILE, 128))


def kept(stats, name, rows):
    return stats[STATS.index(name), rows, :][:, 0:1]


def gate_tile(t, keys, values, hidden, gated, gnorm, stats):
    rows = row_tile(t)
    kk = jnp.zeros((TILE, CB), F32)
    hh, hk = kk, kk
    for b in BLOCKS:
        key = keys[b, rows, :]
        hid = hidden[rows, lanes(b)].astype(F32)
        kk, hh, hk = kk + key * key, hh + hid * hid, hk + hid * key
    key_scale = mean_scale(jnp.sum(kk, axis=1, keepdims=True))
    hidden_scale = mean_scale(jnp.sum(hh, axis=1, keepdims=True))
    score = jnp.sum(hk, axis=1, keepdims=True) * key_scale * hidden_scale
    gate = jax.nn.sigmoid(score / D**0.5)
    gg = jnp.zeros((TILE, CB), F32)
    for b in BLOCKS:
        rounded = (gate * values[b, rows, :]).astype(BF16)
        gated[rows, lanes(b)] = rounded
        gg = gg + rounded.astype(F32) * rounded.astype(F32)
    scale = mean_scale(jnp.sum(gg, axis=1, keepdims=True))
    own = pl.ds(pl.multiple_of(PAD + t * TILE, TILE), TILE)
    for b in BLOCKS:
        gnorm[own, lanes(b)] = gated[rows, lanes(b)].astype(F32) * scale
    for name, value in zip(STATS, (key_scale, hidden_scale, score, gate, scale)):
        keep(stats, name, rows, value)


def same_docs(docs, t, sign):
    window = docs[pl.ds(pl.multiple_of(t * TILE, TILE), 3 * TILE), :][:, 0:1]
    center = window[TILE : 2 * TILE]
    shifted = [window[TILE + sign * DILATION_STEP * j : 2 * TILE + sign * DILATION_STEP * j] for j in range(TAPS)]
    return [center == other for other in shifted]


def conv_tile(t, docs, taps, gnorm, gated, grad, cgrad, out):
    rows = row_tile(t)
    masks = same_docs(docs, t, -1)
    both = pl.ds(pl.multiple_of(t * TILE, TILE), 2 * TILE)
    for b in BLOCKS:
        window = gnorm[both, lanes(b)]
        conv = taps[0:1, lanes(b)] * window[TILE:]
        for j in range(1, TAPS):
            low = TILE - DILATION_STEP * j
            conv = conv + jnp.where(masks[j], taps[j : j + 1, lanes(b)] * window[low : low + TILE], 0.0)
        sig = jax.nn.sigmoid(conv)
        out[rows, lanes(b)] = (conv * sig + gated[rows, lanes(b)].astype(F32)).astype(BF16)
        cgrad[rows, lanes(b)] = grad[rows, lanes(b)].astype(F32) * sig * (1.0 + conv * (1.0 - sig))


def grad_tile(t, docs, taps, gnorm, cgrad, grad, keys, values, hidden, stats, ngrad, key_grad, value_grad):
    rows = row_tile(t)
    masks = same_docs(docs, t, 1)
    both = pl.ds(pl.multiple_of(t * TILE, TILE), 2 * TILE)
    own = pl.ds(pl.multiple_of(PAD + t * TILE, TILE), TILE)
    dots = jnp.zeros((TILE, CB), F32)
    for b in BLOCKS:
        window = cgrad[both, lanes(b)]
        total = taps[0:1, lanes(b)] * window[:TILE]
        for j in range(1, TAPS):
            low = DILATION_STEP * j
            total = total + jnp.where(masks[j], taps[j : j + 1, lanes(b)] * window[low : low + TILE], 0.0)
        ngrad[:, lanes(b)] = total
        dots = dots + gnorm[own, lanes(b)] * total
    mean = jnp.sum(dots, axis=1, keepdims=True) / D
    key_scale, hidden_scale, score, gate, scale = [kept(stats, name, rows) for name in STATS]
    dots = jnp.zeros((TILE, CB), F32)
    for b in BLOCKS:
        total = grad[rows, lanes(b)].astype(F32) + scale * (ngrad[:, lanes(b)] - gnorm[own, lanes(b)] * mean)
        value_grad[rows, lanes(b)] = (total * gate).astype(BF16)
        dots = dots + total * values[b, rows, :]
    score_grad = gate * (1.0 - gate) * jnp.sum(dots, axis=1, keepdims=True)
    front = key_scale * score_grad / D**0.5
    by_hidden, by_key = front * hidden_scale, front * (key_scale * score / D)
    for b in BLOCKS:
        target = by_hidden * hidden[rows, lanes(b)].astype(F32) - by_key * keys[b, rows, :]
        key_grad[rows, lanes(b)] = target.astype(BF16)


def adamw(current, moment, second, gradient):
    moment_new = BETA_ONE * moment + (1.0 - BETA_ONE) * gradient
    second_new = BETA_TWO * second + (1.0 - BETA_TWO) * gradient * gradient
    first_hat = moment_new / (1.0 - BETA_ONE**STEP_COUNT)
    second_hat = second_new / (1.0 - BETA_TWO**STEP_COUNT)
    updated = current - LEARN_RATE * (first_hat / (jnp.sqrt(second_hat) + ADAM_EPS) + DECAY_RATE * current)
    return updated, moment_new, second_new


def kernel(
    owner_ref, local_ref, expand_ref, lengths_ref, taps_ref, table_ref, m_ref, v_ref, hidden_ref, grad_ref, wk_ref, wv_ref,
    memory_out_ref, table_out, m_out, v_out,
    weights, tab, req_out, req_in, reply, fetched, slots, arrived, partial, give, take,
    spread, spread_t, serve, serve_t, docs, memory, keys, values, hidden, grad, gated, gnorm, cgrad, ngrad, stats,
    key_grad, value_grad, out, halo_out, halo_in,
    load_sem, in_sem, req_send, req_recv, rep_send, rep_recv, tz_send, tz_recv, wz_send, wz_recv,
    xy_send, xy_recv, core_send, core_recv, halo_send, halo_recv, slot_send, slot_recv, ring_send, ring_recv,
):
    here = Here()
    greeted = greet(here)
    loads = []
    for b in range(NB):
        src = wk_ref if b < NB // 2 else wv_ref
        loads.append(pltpu.make_async_copy(src.at[:, pl.ds(lanes(b).start, CB)], weights.at[b, here.z, here.core], load_sem.at[b]))
    inputs = [pltpu.make_async_copy(hidden_ref, hidden, in_sem.at[0]), pltpu.make_async_copy(grad_ref, grad, in_sem.at[1])]
    for load in loads + inputs:
        load.start()
    for c in range(NC):
        tab[c, here.z, 0:R_DEV, :] = table_ref[:, c * CW : (c + 1) * CW].astype(BF16)
        tab[c, here.z, R_DEV:TROWS, :] = jnp.zeros((TROWS - R_DEV, CW), BF16)
    plan_slots(owner_ref, local_ref, expand_ref, spread, spread_t, req_out)
    greeted()

    tables = [Ring(here, lambda zz, c=c: tab.at[c, zz], tz_send.at[c], tz_recv.at[c], c % 2) for c in range(NC)]
    blocks = [here.x, NB // 2 + here.y, NB // 2 - 1, NB - 1]
    pieces = [
        Ring(here, lambda zz, b=b: weights.at[b, zz, here.core], wz_send.at[i], wz_recv.at[i], i % 2)
        for i, b in enumerate(blocks)
    ]
    crosses = [
        Cross(here, "x", weights, 0, xy_send.at[0], xy_recv.at[0]),
        Cross(here, "y", weights, NB // 2, xy_send.at[1], xy_recv.at[1]),
    ]
    zeds = [here.zed(step) for step in (0, -1, 1, -2, 2, -3, 3, 4)]
    for ring in tables:
        ring.start(1)
    send_mates(here, req_out, req_in, req_send, req_recv)
    req_in[here.plane] = req_out[here.plane]
    for load in loads:
        load.wait()
    plan_docs(here, lengths_ref, docs)
    for step in (2, 3, 4):
        for ring in tables:
            ring.arrived(step - 1)
            ring.start(step)
        if step == 2:
            mates_arrived(here, req_in, req_recv)
            plan_serve(req_in, serve, serve_t)
        if step == 3:
            for ring in pieces[:2]:
                ring.start(1)
    for c in range(NC):
        tables[c].arrived(4)
        rows = nn(serve[...], tab[c].reshape(Z * TROWS, CW))
        reply[c] = rows.astype(BF16).reshape(PLANE, MSG, CW)
        fetched[c, here.plane] = reply[c, here.plane]
        send_mates(here, reply.at[c], fetched.at[c], rep_send.at[c], rep_recv.at[c])

    def to_partner(b):
        ref = weights.at[b, :, here.core]
        return remote(ref, ref, core_send.at[b], core_recv.at[b], here.partner())

    def from_partner(b):
        ref = weights.at[b, :, 1 - here.core]
        remote(ref, ref, core_send.at[b], core_recv.at[b], here.partner()).wait_recv()

    seen = relayed = 1
    for step in (1, 2, 3, 4):
        for ring in pieces[:2]:
            ring.arrived(step)
            if step < 4:
                ring.start(step + 1)
        if step == 4:
            for ring in pieces[2:]:
                ring.start(1)
        upto = min(Z, seen + 2)
        for i in range(seen, upto):
            for cross in crosses:
                cross.start(zeds[i], i)
        for i in range(relayed, seen):
            for cross in crosses:
                cross.relay(zeds[i], i)
        relayed, seen = seen, upto
    for b in (here.x, NB // 2 + here.y):
        to_partner(b).start()

    def project(b):
        from_partner(b)
        return nn(memory[...], weights[b].reshape(E, CB))

    def project_key(b):
        keys[b] = project(b)

    def project_value(b):
        values[b] = project(NB // 2 + b)

    for i in range(relayed, Z):
        for cross in crosses:
            cross.relay(zeds[i], i)
    for step in (-1, 1):
        to_partner(here.exx(step)).start()
        to_partner(NB // 2 + here.wye(step)).start()
    for ring in pieces[2:]:
        ring.arrived(1)
        ring.start(2)
    for c in range(NC):
        mates_arrived(here, fetched.at[c], rep_recv.at[c])
        memory[:, c * CW : (c + 1) * CW] = nn(spread[...], fetched[c].reshape(PLACES, CW)).astype(BF16)
    project_key(here.x)
    project_value(here.y)
    for ring in pieces[2:]:
        ring.arrived(2)
        ring.start(3)
    for step in (-1, 1):
        project_key(here.exx(step))
        project_value(here.wye(step))
    for i in range(1, Z):
        for cross in crosses:
            cross.finish(zeds[i], i)
    to_partner(here.exx(2)).start()
    to_partner(NB // 2 + here.wye(2)).start()
    for ring in pieces[2:]:
        ring.arrived(3)
        ring.start(4)
    project_key(here.exx(2))
    project_value(here.wye(2))
    for ring in pieces[2:]:
        ring.arrived(4)
    to_partner(NB // 2 - 1).start()
    to_partner(NB - 1).start()
    for load in inputs:
        load.wait()
    project_key(NB // 2 - 1)
    project_value(NB // 2 - 1)

    def halo(way):
        sign = 1 if way == 0 else -1
        device = (here.row, lax.rem(here.col + sign + X * Y, X * Y))
        return remote(halo_out.at[way], halo_in.at[way], halo_send.at[way], halo_recv.at[way], device)

    last = TOK // TILE - 1

    def gate_step(t, carry):
        gate_tile(t, keys, values, hidden, gated, gnorm, stats)
        return carry

    gate_tile(last, keys, values, hidden, gated, gnorm, stats)
    halo_out[0] = gated[TOK - TILE : TOK, :]
    halo(0).start()
    lax.fori_loop(0, last, gate_step, 0)
    halo(0).wait_recv()
    total = jnp.zeros((TILE, CB), F32)
    for b in BLOCKS:
        rows = halo_in[0, :, lanes(b)].astype(F32)
        total = total + rows * rows
    scale = mean_scale(jnp.sum(total, axis=1, keepdims=True))
    for b in BLOCKS:
        gnorm[0:PAD, lanes(b)] = halo_in[0, :, lanes(b)].astype(F32) * scale

    def conv_step(t, carry):
        conv_tile(t, docs, taps_ref, gnorm, gated, grad, cgrad, out)
        return carry

    conv_tile(0, docs, taps_ref, gnorm, gated, grad, cgrad, out)
    halo_out[1] = cgrad[0:TILE, :].astype(BF16)
    halo(1).start()
    lax.fori_loop(1, last + 1, conv_step, 0)
    out_copy = pltpu.make_async_copy(out, memory_out_ref, in_sem.at[2])
    out_copy.start()

    def grad_step(t, carry):
        grad_tile(t, docs, taps_ref, gnorm, cgrad, grad, keys, values, hidden, stats, ngrad, key_grad, value_grad)
        return carry

    lax.fori_loop(0, last, grad_step, 0)
    halo(1).wait_recv()
    cgrad[TOK : TOK + PAD, :] = halo_in[1].astype(F32)
    grad_step(last, 0)

    for c in range(NC):
        first, stop = c * CW // (2 * WROWS), -(-(c + 1) * CW // (2 * WROWS))
        skip = c * CW - first * 2 * WROWS
        total = jnp.zeros((TOK, CW), F32)
        for b in range(NB):
            part = weights[b, first:stop].reshape((stop - first) * 2 * WROWS, CB)[skip : skip + CW]
            source = key_grad if b < NB // 2 else value_grad
            total = total + nt(source[:, lanes(b)], part)
        slots[c] = nn(spread_t[...], total.astype(BF16)).astype(BF16).reshape(PLANE, MSG, CW)
        arrived[c, here.plane] = slots[c, here.plane]
        send_mates(here, slots.at[c], arrived.at[c], slot_send.at[c], slot_recv.at[c])

    def hop(c, way, step):
        sign = 1 if way == 0 else -1
        return remote(
            give.at[c, way, step - 1], take.at[c, way, step - 1],
            ring_send.at[c, way, step - 1], ring_recv.at[c, way, step - 1], here.at_z(sign),
        )

    def length(c, way):
        return Z // 2 if way == c % 2 else Z // 2 - 1

    def advance(c, step):
        for way in range(2):
            final = length(c, way)
            if step > final:
                continue
            sign = 1 if way == 0 else -1
            mine = partial[c, here.zed(sign * (final - step + 1))]
            if step > 1:
                hop(c, way, step - 1).wait_recv()
                mine = mine + take[c, way, step - 2].astype(F32)
            give[c, way, step - 1] = mine.astype(BF16)
            hop(c, way, step).start()

    def finish(c):
        total = partial[c, here.z]
        for way in range(2):
            final = length(c, way)
            hop(c, way, final).wait_recv()
            total = total + take[c, way, final - 1].astype(F32)
        cols = slice(c * CW, (c + 1) * CW)
        new_t, new_m, new_v = adamw(table_ref[:, cols], m_ref[:, cols], v_ref[:, cols], total[:R_DEV])
        table_out[:, cols] = new_t
        m_out[:, cols] = new_m
        v_out[:, cols] = new_v

    for c in range(NC):
        mates_arrived(here, arrived.at[c], slot_recv.at[c])
        partial[c] = nn(serve_t[...], arrived[c].reshape(PLACES, CW)).reshape(Z, TROWS, CW)
        advance(c, 1)
        for back in range(1, min(c, 3) + 1):
            advance(c - back, back + 1)
    for step in range(2, 5):
        for c in range(NC):
            if c + step > NC:
                advance(c, step)
    for c in range(NC):
        finish(c)

    out_copy.wait()
    for b in range(NB):
        to_partner(b).wait_send()
    for ring in tables + pieces:
        ring.drain()
    for i in range(1, Z):
        for cross in crosses:
            cross.drain(zeds[i], i)
    for way in range(2):
        halo(way).wait_send()
    mates_sent(here, req_out, req_send)
    for c in range(NC):
        mates_sent(here, reply.at[c], rep_send.at[c])
        mates_sent(here, slots.at[c], slot_send.at[c])
        for way in range(2):
            for step in range(1, length(c, way) + 1):
                hop(c, way, step).wait_send()


def on_device(
    hidden, grad_out, w_key, w_value, depthwise_weight, table, adam_m, adam_v,
    row_owner, row_local, expand_index, doc_lengths,
):
    vmem = pl.BlockSpec(memory_space=pltpu.VMEM)
    any_ = pl.BlockSpec(memory_space=pl.ANY)
    dma = pltpu.SemaphoreType.DMA
    rows = (NC, PLANE, MSG, CW)
    hops = (NC, 2, Z // 2)
    row_out = jax.ShapeDtypeStruct((R_DEV, E), F32)
    memory_out, new_table, new_moment, new_second = pl.pallas_call(
        kernel,
        out_shape=(jax.ShapeDtypeStruct((TOK, D), BF16), row_out, row_out, row_out),
        in_specs=[vmem] * 8 + [any_] * 4,
        out_specs=(any_, vmem, vmem, vmem),
        scratch_shapes=[
            pltpu.VMEM((NB, Z, 2, WROWS, CB), BF16),
            pltpu.VMEM((NC, Z, TROWS, CW), BF16),
            pltpu.VMEM((PLANE, 1, 128), F32),
            pltpu.VMEM((PLANE, 1, 128), F32),
            pltpu.VMEM(rows, BF16),
            pltpu.VMEM(rows, BF16),
            pltpu.VMEM(rows, BF16),
            pltpu.VMEM(rows, BF16),
            pltpu.VMEM((NC, Z, TROWS, CW), F32),
            pltpu.VMEM(hops + (TROWS, CW), BF16),
            pltpu.VMEM(hops + (TROWS, CW), BF16),
            pltpu.VMEM((TOK, PLACES), BF16),
            pltpu.VMEM((PLACES, TOK), BF16),
            pltpu.VMEM((PLACES, Z * TROWS), BF16),
            pltpu.VMEM((Z * TROWS, PLACES), BF16),
            pltpu.VMEM((TOK + 2 * PAD, 128), F32),
            pltpu.VMEM((TOK, E), BF16),
            pltpu.VMEM((NB // 2, TOK, CB), F32),
            pltpu.VMEM((NB // 2, TOK, CB), F32),
            pltpu.VMEM((TOK, D), BF16),
            pltpu.VMEM((TOK, D), BF16),
            pltpu.VMEM((TOK, D), BF16),
            pltpu.VMEM((PAD + TOK, D), F32),
            pltpu.VMEM((TOK + PAD, D), F32),
            pltpu.VMEM((TILE, D), F32),
            pltpu.VMEM((len(STATS), TOK, 128), F32),
            pltpu.VMEM((TOK, D), BF16),
            pltpu.VMEM((TOK, D), BF16),
            pltpu.VMEM((TOK, D), BF16),
            pltpu.VMEM((2, TILE, D), BF16),
            pltpu.VMEM((2, TILE, D), BF16),
            dma((NB,)), dma((3,)), dma, dma, dma((NC,)), dma((NC,)),
            dma(hops), dma(hops), dma((4, 2, Z // 2)), dma((4, 2, Z // 2)),
            dma((2, 4, Z)), dma((2, 4, Z)), dma((NB,)), dma((NB,)),
            dma((2,)), dma((2,)), dma((NC,)), dma((NC,)), dma(hops), dma(hops),
        ],
        compiler_params=pltpu.CompilerParams(
            collective_id=0, has_side_effects=True, vmem_limit_bytes=56 * 1024 * 1024
        ),
        name="memory_branch",
    )(
        row_owner.reshape(1, U), row_local, expand_index[0].T, doc_lengths, depthwise_weight,
        table, adam_m, adam_v, hidden[0], grad_out[0], w_key, w_value,
    )
    return (memory_out[None], new_table, new_moment, new_second)


def solution(mesh):
    placed = (
        P("row", "col", None),
        P("row", "col", None),
        P("row", None),
        P("row", None),
        P(),
        P(("row", "col"), None),
        P(("row", "col"), None),
        P(("row", "col"), None),
        P("row", "col", None),
        P("row", "col"),
        P("row", "col", None),
        P("row", None),
    )
    return jax.shard_map(
        on_device,
        mesh=mesh,
        in_specs=placed,
        out_specs=(
            P("row", "col", None),
            P(("row", "col"), None),
            P(("row", "col"), None),
            P(("row", "col"), None),
        ),
        check_vma=False,
    )
```

time: 158 us -> 129 us (0.82)
  the two profiles are of different devices: /device:TPU:34 before, /device:TPU:1 now
where the time goes in v2:
time: 129 us
  Pallas kernels  123 us (95%)
  local copies, waits for them, and re-layouts  4.7 us (4%)
    pallas_call x1, Pallas kernels, on_device(): pl.pallas_call(kernel, out_shape=(jax.ShapeDtypeStruct((TOK, D), BF16), r...  123 us
    unnamed x10, local copies, waits for them, and re-layouts  4.7 us

profile of v2, /device:TPU:1, one launch (start us, length us, event | category | flops | bytes accessed | tf_op | source)
XLA Modules:
  0.0 128.6 jit_solution(9826438527350125026)
XLA Ops:
  0.6 123.2 %memory_branch.1 = (bf16[128,2560]{1,0:T(8,128)(2,1)}, f32[40,1280]{1,0:T(8,128)}, f32[40,1280]{1,0:T(8,128)}, f32[40,1280]{1,0:T(8,128)}) custom-call(s32[1,144]{1,0:T(1,128)} %bitcast.10, s32[1,144]{1,0:T(1,128)} %local_ref.1, s32[2,128]{1,0:T(2,128)} %bitcast.11, s32[1,8]{1,0:T(1,128)} %lengths_ref.1, f32[4,2560]{1,0:T(4,128)} %taps_ref.1, ...), custom_call_target="tpu_custom_call" | custom-call | tf_op jit(solution)/shard_map/memory_branch/pallas_call | solution.py:643
  123.9 0.0 copy-start.2
  123.9 2.0 %copy.20 = bf16[1,128,2560]{2,1,0:T(8,128)(2,1)} copy(bf16[1,128,2560]{2,1,0:T(8,128)(2,1)} %bitcast.7) | data formatting | bytes 1310720
  125.9 0.0 copy-done.2
  125.9 0.0 copy-start.1
  125.9 0.7 copy.21
  126.6 0.3 copy-done.1
  126.9 0.0 copy-start
  126.9 0.7 copy.22
  127.6 0.3 copy-done
  127.9 0.7 copy.23
Async XLA Ops:
  123.9 2.0 %copy-start.2 = (f32[40,1280]{1,0:T(8,128)S(1)}, f32[40,1280]{1,0:T(8,128)}, u32[]{:S(2)}) copy-start(f32[40,1280]{1,0:T(8,128)} %get-tuple-element.17) | copy-start | bytes 614404
  125.9 1.0 copy-start.1
  126.9 1.0 copy-start

commit v3 on v2

--- a/solution.py
+++ b/solution.py
@@ -20,6 +20,7 @@
 TOK, U, R_DEV = 128, 144, 40
 CW = 256
 NC = E // CW
+RINGS = 3
 TROWS = 48
 MSG = 2 * Z
 PLACES = PLANE * MSG
@@ -85,9 +86,9 @@
         return carry
 
     lax.fori_loop(1, PLANE, one, 0)
-    for step in (1, -1):
+    for step in range(1, Z):
         pl.semaphore_signal(barrier, inc=1, device_id=here.at_z(step), device_id_type=MESH)
-    return lambda: pl.semaphore_wait(barrier, PLANE + 1)
+    return lambda: pl.semaphore_wait(barrier, PLANE - 1 + Z - 1)
 
 
 def iota(shape, dim):
@@ -283,7 +284,11 @@
 
 
 def kept(stats, name, rows):
-    return stats[STATS.index(name), rows, :][:, 0:1]
+    return wide(stats[STATS.index(name), rows, :])
+
+
+def wide(value):
+    return jnp.concatenate([value] * (CB // 128), axis=1)
 
 
 def gate_tile(t, keys, values, hidden, gated, gnorm, stats):
@@ -312,10 +317,10 @@
 
 
 def same_docs(docs, t, sign):
-    window = docs[pl.ds(pl.multiple_of(t * TILE, TILE), 3 * TILE), :][:, 0:1]
+    window = docs[pl.ds(pl.multiple_of(t * TILE, TILE), 3 * TILE), :]
     center = window[TILE : 2 * TILE]
     shifted = [window[TILE + sign * DILATION_STEP * j : 2 * TILE + sign * DILATION_STEP * j] for j in range(TAPS)]
-    return [center == other for other in shifted]
+    return [wide(jnp.where(center == other, 1.0, 0.0)) for other in shifted]
 
 
 def conv_tile(t, docs, taps, gnorm, gated, grad, cgrad, out):
@@ -327,7 +332,7 @@
         conv = taps[0:1, lanes(b)] * window[TILE:]
         for j in range(1, TAPS):
             low = TILE - DILATION_STEP * j
-            conv = conv + jnp.where(masks[j], taps[j : j + 1, lanes(b)] * window[low : low + TILE], 0.0)
+            conv = conv + masks[j] * (taps[j : j + 1, lanes(b)] * window[low : low + TILE])
         sig = jax.nn.sigmoid(conv)
         out[rows, lanes(b)] = (conv * sig + gated[rows, lanes(b)].astype(F32)).astype(BF16)
         cgrad[rows, lanes(b)] = grad[rows, lanes(b)].astype(F32) * sig * (1.0 + conv * (1.0 - sig))
@@ -344,7 +349,7 @@
         total = taps[0:1, lanes(b)] * window[:TILE]
         for j in range(1, TAPS):
             low = DILATION_STEP * j
-            total = total + jnp.where(masks[j], taps[j : j + 1, lanes(b)] * window[low : low + TILE], 0.0)
+            total = total + masks[j] * (taps[j : j + 1, lanes(b)] * window[low : low + TILE])
         ngrad[:, lanes(b)] = total
         dots = dots + gnorm[own, lanes(b)] * total
     mean = jnp.sum(dots, axis=1, keepdims=True) / D
@@ -372,13 +377,14 @@
 
 
 def kernel(
-    owner_ref, local_ref, expand_ref, lengths_ref, taps_ref, table_ref, m_ref, v_ref, hidden_ref, grad_ref, wk_ref, wv_ref,
-    memory_out_ref, table_out, m_out, v_out,
+    owner_ref, local_ref, expand_ref, lengths_ref, taps_ref, table_ref, hidden_ref, grad_ref, wk_ref, wv_ref,
+    out, row_grad,
     weights, tab, req_out, req_in, reply, fetched, slots, arrived, partial, give, take,
     spread, spread_t, serve, serve_t, docs, memory, keys, values, hidden, grad, gated, gnorm, cgrad, ngrad, stats,
-    key_grad, value_grad, out, halo_out, halo_in,
+    key_grad, value_grad, grads_t, halo_out, halo_in, give_far, take_far,
     load_sem, in_sem, req_send, req_recv, rep_send, rep_recv, tz_send, tz_recv, wz_send, wz_recv,
     xy_send, xy_recv, core_send, core_recv, halo_send, halo_recv, slot_send, slot_recv, ring_send, ring_recv,
+    far_send, far_recv,
 ):
     here = Here()
     greeted = greet(here)
@@ -406,23 +412,38 @@
         Cross(here, "y", weights, NB // 2, xy_send.at[1], xy_recv.at[1]),
     ]
     zeds = [here.zed(step) for step in (0, -1, 1, -2, 2, -3, 3, 4)]
+    for load in loads:
+        load.wait()
     for ring in tables:
+        ring.start(1)
+    for ring in pieces[:2]:
         ring.start(1)
     send_mates(here, req_out, req_in, req_send, req_recv)
     req_in[here.plane] = req_out[here.plane]
-    for load in loads:
-        load.wait()
     plan_docs(here, lengths_ref, docs)
-    for step in (2, 3, 4):
+    for step in (1, 2, 3):
         for ring in tables:
-            ring.arrived(step - 1)
-            ring.start(step)
-        if step == 2:
+            ring.arrived(step)
+            ring.start(step + 1)
+        for ring in pieces[:2]:
+            ring.arrived(step)
+            ring.start(step + 1)
+        for cross in crosses:
+            for i in (2 * step - 1, 2 * step):
+                cross.start(zeds[i], i)
+        if step == 1:
             mates_arrived(here, req_in, req_recv)
             plan_serve(req_in, serve, serve_t)
-        if step == 3:
-            for ring in pieces[:2]:
-                ring.start(1)
+        if step > 1:
+            for cross in crosses:
+                for i in (2 * step - 3, 2 * step - 2):
+                    cross.relay(zeds[i], i)
+    for ring in pieces[2:]:
+        ring.start(1)
+    for ring in pieces[:2]:
+        ring.arrived(4)
+    for cross in crosses:
+        cross.start(zeds[Z - 1], Z - 1)
     for c in range(NC):
         tables[c].arrived(4)
         rows = nn(serve[...], tab[c].reshape(Z * TROWS, CW))
@@ -438,26 +459,6 @@
         ref = weights.at[b, :, 1 - here.core]
         remote(ref, ref, core_send.at[b], core_recv.at[b], here.partner()).wait_recv()
 
-    seen = relayed = 1
-    for step in (1, 2, 3, 4):
-        for ring in pieces[:2]:
-            ring.arrived(step)
-            if step < 4:
-                ring.start(step + 1)
-        if step == 4:
-            for ring in pieces[2:]:
-                ring.start(1)
-        upto = min(Z, seen + 2)
-        for i in range(seen, upto):
-            for cross in crosses:
-                cross.start(zeds[i], i)
-        for i in range(relayed, seen):
-            for cross in crosses:
-                cross.relay(zeds[i], i)
-        relayed, seen = seen, upto
-    for b in (here.x, NB // 2 + here.y):
-        to_partner(b).start()
-
     def project(b):
         from_partner(b)
         return nn(memory[...], weights[b].reshape(E, CB))
@@ -468,42 +469,42 @@
     def project_value(b):
         values[b] = project(NB // 2 + b)
 
-    for i in range(relayed, Z):
-        for cross in crosses:
+    for b in (here.x, NB // 2 + here.y):
+        to_partner(b).start()
+    for ring in pieces[2:]:
+        ring.arrived(1)
+        ring.start(2)
+    for cross in crosses:
+        for i in (Z - 3, Z - 2):
             cross.relay(zeds[i], i)
+    for step in (2, 3):
+        for ring in pieces[2:]:
+            ring.arrived(step)
+            ring.start(step + 1)
+    for load in inputs:
+        load.wait()
+    for cross in crosses:
+        cross.relay(zeds[Z - 1], Z - 1)
     for step in (-1, 1):
         to_partner(here.exx(step)).start()
         to_partner(NB // 2 + here.wye(step)).start()
-    for ring in pieces[2:]:
-        ring.arrived(1)
-        ring.start(2)
     for c in range(NC):
         mates_arrived(here, fetched.at[c], rep_recv.at[c])
         memory[:, c * CW : (c + 1) * CW] = nn(spread[...], fetched[c].reshape(PLACES, CW)).astype(BF16)
     project_key(here.x)
     project_value(here.y)
-    for ring in pieces[2:]:
-        ring.arrived(2)
-        ring.start(3)
-    for step in (-1, 1):
-        project_key(here.exx(step))
-        project_value(here.wye(step))
     for i in range(1, Z):
         for cross in crosses:
             cross.finish(zeds[i], i)
     to_partner(here.exx(2)).start()
     to_partner(NB // 2 + here.wye(2)).start()
     for ring in pieces[2:]:
-        ring.arrived(3)
-        ring.start(4)
-    project_key(here.exx(2))
-    project_value(here.wye(2))
-    for ring in pieces[2:]:
         ring.arrived(4)
     to_partner(NB // 2 - 1).start()
     to_partner(NB - 1).start()
-    for load in inputs:
-        load.wait()
+    for step in (-1, 1, 2):
+        project_key(here.exx(step))
+        project_value(here.wye(step))
     project_key(NB // 2 - 1)
     project_value(NB // 2 - 1)
 
@@ -539,8 +540,6 @@
     halo_out[1] = cgrad[0:TILE, :].astype(BF16)
     halo(1).start()
     lax.fori_loop(1, last + 1, conv_step, 0)
-    out_copy = pltpu.make_async_copy(out, memory_out_ref, in_sem.at[2])
-    out_copy.start()
 
     def grad_step(t, carry):
         grad_tile(t, docs, taps_ref, gnorm, cgrad, grad, keys, values, hidden, stats, ngrad, key_grad, value_grad)
@@ -551,15 +550,17 @@
     cgrad[TOK : TOK + PAD, :] = halo_in[1].astype(F32)
     grad_step(last, 0)
 
+    for b in range(NB):
+        source = key_grad if b < NB // 2 else value_grad
+        grads_t[b] = source[:, lanes(b)].T
     for c in range(NC):
         first, stop = c * CW // (2 * WROWS), -(-(c + 1) * CW // (2 * WROWS))
         skip = c * CW - first * 2 * WROWS
-        total = jnp.zeros((TOK, CW), F32)
+        total = jnp.zeros((CW, TOK), F32)
         for b in range(NB):
             part = weights[b, first:stop].reshape((stop - first) * 2 * WROWS, CB)[skip : skip + CW]
-            source = key_grad if b < NB // 2 else value_grad
-            total = total + nt(source[:, lanes(b)], part)
-        slots[c] = nn(spread_t[...], total.astype(BF16)).astype(BF16).reshape(PLANE, MSG, CW)
+            total = total + nn(part, grads_t[b])
+        slots[c] = nt(spread_t[...], total.astype(BF16)).astype(BF16).reshape(PLANE, MSG, CW)
         arrived[c, here.plane] = slots[c, here.plane]
         send_mates(here, slots.at[c], arrived.at[c], slot_send.at[c], slot_recv.at[c])
 
@@ -586,32 +587,48 @@
             give[c, way, step - 1] = mine.astype(BF16)
             hop(c, way, step).start()
 
+    def far(c, step):
+        place = c - RINGS
+        return remote(
+            give_far.at[place, here.zed(step)], take_far.at[place, step],
+            far_send.at[place, step], far_recv.at[place, step], here.at_z(step),
+        )
+
+    def send_far(c):
+        give_far[c - RINGS] = partial[c].astype(BF16)
+        for step in range(1, Z):
+            far(c, step).start()
+
     def finish(c):
         total = partial[c, here.z]
-        for way in range(2):
-            final = length(c, way)
-            hop(c, way, final).wait_recv()
-            total = total + take[c, way, final - 1].astype(F32)
-        cols = slice(c * CW, (c + 1) * CW)
-        new_t, new_m, new_v = adamw(table_ref[:, cols], m_ref[:, cols], v_ref[:, cols], total[:R_DEV])
-        table_out[:, cols] = new_t
-        m_out[:, cols] = new_m
-        v_out[:, cols] = new_v
+        if c < RINGS:
+            for way in range(2):
+                final = length(c, way)
+                hop(c, way, final).wait_recv()
+                total = total + take[c, way, final - 1].astype(F32)
+        else:
+            for step in range(1, Z):
+                far(c, step).wait_recv()
+                total = total + take_far[c - RINGS, step].astype(F32)
+        row_grad[:, c * CW : (c + 1) * CW] = total[:R_DEV]
 
     for c in range(NC):
         mates_arrived(here, arrived.at[c], slot_recv.at[c])
         partial[c] = nn(serve_t[...], arrived[c].reshape(PLACES, CW)).reshape(Z, TROWS, CW)
-        advance(c, 1)
-        for back in range(1, min(c, 3) + 1):
-            advance(c - back, back + 1)
-    for step in range(2, 5):
-        for c in range(NC):
+        if c < RINGS:
+            advance(c, 1)
+        else:
+            send_far(c)
+        for back in range(1, 4):
+            if 0 <= c - back < RINGS:
+                advance(c - back, back + 1)
+    for step in range(2, Z // 2 + 1):
+        for c in range(RINGS):
             if c + step > NC:
                 advance(c, step)
     for c in range(NC):
         finish(c)
 
-    out_copy.wait()
     for b in range(NB):
         to_partner(b).wait_send()
     for ring in tables + pieces:
@@ -625,9 +642,13 @@
     for c in range(NC):
         mates_sent(here, reply.at[c], rep_send.at[c])
         mates_sent(here, slots.at[c], slot_send.at[c])
-        for way in range(2):
-            for step in range(1, length(c, way) + 1):
-                hop(c, way, step).wait_send()
+        if c < RINGS:
+            for way in range(2):
+                for step in range(1, length(c, way) + 1):
+                    hop(c, way, step).wait_send()
+        else:
+            for step in range(1, Z):
+                far(c, step).wait_send()
 
 
 def on_device(
@@ -638,13 +659,13 @@
     any_ = pl.BlockSpec(memory_space=pl.ANY)
     dma = pltpu.SemaphoreType.DMA
     rows = (NC, PLANE, MSG, CW)
-    hops = (NC, 2, Z // 2)
-    row_out = jax.ShapeDtypeStruct((R_DEV, E), F32)
-    memory_out, new_table, new_moment, new_second = pl.pallas_call(
+    hops = (RINGS, 2, Z // 2)
+    fars = (NC - RINGS, Z)
+    memory_out, row_grad = pl.pallas_call(
         kernel,
-        out_shape=(jax.ShapeDtypeStruct((TOK, D), BF16), row_out, row_out, row_out),
-        in_specs=[vmem] * 8 + [any_] * 4,
-        out_specs=(any_, vmem, vmem, vmem),
+        out_shape=(jax.ShapeDtypeStruct((TOK, D), BF16), jax.ShapeDtypeStruct((R_DEV, E), F32)),
+        in_specs=[vmem] * 6 + [any_] * 4,
+        out_specs=(vmem, vmem),
         scratch_shapes=[
             pltpu.VMEM((NB, Z, 2, WROWS, CB), BF16),
             pltpu.VMEM((NC, Z, TROWS, CW), BF16),
@@ -674,13 +695,15 @@
             pltpu.VMEM((len(STATS), TOK, 128), F32),
             pltpu.VMEM((TOK, D), BF16),
             pltpu.VMEM((TOK, D), BF16),
-            pltpu.VMEM((TOK, D), BF16),
+            pltpu.VMEM((NB, CB, TOK), BF16),
             pltpu.VMEM((2, TILE, D), BF16),
             pltpu.VMEM((2, TILE, D), BF16),
-            dma((NB,)), dma((3,)), dma, dma, dma((NC,)), dma((NC,)),
-            dma(hops), dma(hops), dma((4, 2, Z // 2)), dma((4, 2, Z // 2)),
+            pltpu.VMEM(fars + (TROWS, CW), BF16),
+            pltpu.VMEM(fars + (TROWS, CW), BF16),
+            dma((NB,)), dma((2,)), dma, dma, dma((NC,)), dma((NC,)),
+            dma((NC, 2, Z // 2)), dma((NC, 2, Z // 2)), dma((4, 2, Z // 2)), dma((4, 2, Z // 2)),
             dma((2, 4, Z)), dma((2, 4, Z)), dma((NB,)), dma((NB,)),
-            dma((2,)), dma((2,)), dma((NC,)), dma((NC,)), dma(hops), dma(hops),
+            dma((2,)), dma((2,)), dma((NC,)), dma((NC,)), dma(hops), dma(hops), dma(fars), dma(fars),
         ],
         compiler_params=pltpu.CompilerParams(
             collective_id=0, has_side_effects=True, vmem_limit_bytes=56 * 1024 * 1024
@@ -688,8 +711,9 @@
         name="memory_branch",
     )(
         row_owner.reshape(1, U), row_local, expand_index[0].T, doc_lengths, depthwise_weight,
-        table, adam_m, adam_v, hidden[0], grad_out[0], w_key, w_value,
+        table, hidden[0], grad_out[0], w_key, w_value,
     )
+    new_table, new_moment, new_second = adamw(table, adam_m, adam_v, row_grad)
     return (memory_out[None], new_table, new_moment, new_second)
 
 

time: 129 us -> 112 us (0.87)
  Pallas kernels: 123 us -> 108 us
  local copies, waits for them, and re-layouts: 4.7 us -> 0.85 us
  other arithmetic: 0 us -> 1.91 us
    pallas_call x1, Pallas kernels: 123 us -> 108 us  [on_device(): pl.pallas_call(kernel, out_shape=(jax.ShapeDtypeStruct((TOK, D), BF16), j...]
    unnamed x10 -> x9, local copies, waits for them, and re-layouts: 4.7 us -> 0.85 us
    sub x0 -> x1, other arithmetic: none -> 1.91 us  [adamw(): current - LEARN_RATE * (first_hat / (jnp.sqrt(second_hat) + ADAM_EPS) + D...]
where the time goes in v3:
time: 112 us
  Pallas kernels  108 us (96%)
  other arithmetic  1.91 us (2%)
    pallas_call x1, Pallas kernels, on_device(): pl.pallas_call(kernel, out_shape=(jax.ShapeDtypeStruct((TOK, D), BF16), j...  108 us

profile of v3, /device:TPU:1, one launch (start us, length us, event | category | flops | bytes accessed | tf_op | source)
XLA Modules:
  0.0 111.5 jit_solution(15399366999573598529)
XLA Ops:
  0.6 0.0 copy-start
  0.6 0.0 copy-start.2
  0.7 0.0 copy-start.3
  0.7 108.1 %memory_branch.1 = (bf16[128,2560]{1,0:T(8,128)(2,1)}, f32[40,1280]{1,0:T(8,128)}) custom-call(s32[1,144]{1,0:T(1,128)} %bitcast.10, s32[1,144]{1,0:T(1,128)} %local_ref.1, s32[2,128]{1,0:T(2,128)} %bitcast.11, s32[1,8]{1,0:T(1,128)} %lengths_ref.1, f32[4,2560]{1,0:T(4,128)} %taps_ref.1, f32[40,1280]{1,0:T(8,128)} %table_ref.1, bf16[128,2560]{1,0:T(8,128)(2,1)} %bitcast.8, ...), custom_call_target="tpu_custom_call" | custom-call | tf_op jit(solution)/shard_map/memory_branch/pallas_call | solution.py:664
  108.7 0.0 copy-done
  108.7 0.0 copy-done.2
  108.8 0.0 copy-done.3
  108.8 0.0 copy-start.1
  108.8 1.9 %multiply_subtract_fusion = (f32[40,1280]{1,0:T(8,128)}, f32[40,1280]{1,0:T(8,128)}, f32[40,1280]{1,0:T(8,128)}) fusion(f32[40,1280]{1,0:T(8,128)S(1)} %copy-done, f32[40,1280]{1,0:T(8,128)} %get-tuple-element.7, f32[40,1280]{1,0:T(8,128)S(1)} %copy-done.2, f32[40,1280]{1,0:T(8,128)S(1)} %copy-done.3), kind=kLoop, calls=%fused_computation.2 | loop fusion | flops 768000 | bytes 1433600 | tf_op jit(solution)/shard_map/sub | solution.py:375
  110.7 0.0 copy-done.1
  110.7 0.8 copy.17
Async XLA Ops:
  0.6 108.1 %copy-start = (f32[40,1280]{1,0:T(8,128)S(1)}, f32[40,1280]{1,0:T(8,128)}, u32[]{:S(2)}) copy-start(f32[40,1280]{1,0:T(8,128)} %table_ref.1) | copy-start | bytes 614404
  0.6 108.1 %copy-start.2 = (f32[40,1280]{1,0:T(8,128)S(1)}, f32[40,1280]{1,0:T(8,128)}, u32[]{:S(2)}) copy-start(f32[40,1280]{1,0:T(8,128)} %param.18) | copy-start | bytes 614404
  0.7 108.1 %copy-start.3 = (f32[40,1280]{1,0:T(8,128)S(1)}, f32[40,1280]{1,0:T(8,128)}, u32[]{:S(2)}) copy-start(f32[40,1280]{1,0:T(8,128)} %param.19) | copy-start | bytes 614404
  108.8 1.9 %copy-start.1 = (bf16[128,2560]{1,0:T(8,128)(2,1)S(1)}, bf16[128,2560]{1,0:T(8,128)(2,1)}, u32[]{:S(2)}) copy-start(bf16[128,2560]{1,0:T(8,128)(2,1)} %get-tuple-element.6) | copy-start | bytes 1966084

commit v4 on v3

--- a/solution.py
+++ b/solution.py
@@ -21,6 +21,7 @@
 CW = 256
 NC = E // CW
 RINGS = 3
+AHEAD = 2
 TROWS = 48
 MSG = 2 * Z
 PLACES = PLANE * MSG
@@ -66,6 +67,9 @@
 
     def at_y(self, step):
         return (self.row, self.x * Y + self.wye(step))
+
+    def neighbour(self, step):
+        return (self.row, lax.rem(self.col + step + X * Y, X * Y))
 
     def partner(self):
         return (self.z * 2 + 1 - self.core, self.col)
@@ -215,9 +219,14 @@
                 got.append(-sign * step)
         return got
 
+    def sent(self, step):
+        for way in range(2):
+            if step <= self.steps(way):
+                self.copy(way, step).wait_send()
+
     def drain(self):
         for way in range(2):
-            for step in range(1, self.steps(way) + 1):
+            for step in range(2, self.steps(way) + 1):
                 self.copy(way, step).wait_send()
 
 
@@ -323,7 +332,7 @@
     return [wide(jnp.where(center == other, 1.0, 0.0)) for other in shifted]
 
 
-def conv_tile(t, docs, taps, gnorm, gated, grad, cgrad, out):
+def conv_tile(t, docs, taps, gnorm, gated, grad, cgrad, out=None):
     rows = row_tile(t)
     masks = same_docs(docs, t, -1)
     both = pl.ds(pl.multiple_of(t * TILE, TILE), 2 * TILE)
@@ -334,7 +343,8 @@
             low = TILE - DILATION_STEP * j
             conv = conv + masks[j] * (taps[j : j + 1, lanes(b)] * window[low : low + TILE])
         sig = jax.nn.sigmoid(conv)
-        out[rows, lanes(b)] = (conv * sig + gated[rows, lanes(b)].astype(F32)).astype(BF16)
+        if out is not None:
+            out[rows, lanes(b)] = (conv * sig + gated[rows, lanes(b)].astype(F32)).astype(BF16)
         cgrad[rows, lanes(b)] = grad[rows, lanes(b)].astype(F32) * sig * (1.0 + conv * (1.0 - sig))
 
 
@@ -381,7 +391,7 @@
     out, row_grad,
     weights, tab, req_out, req_in, reply, fetched, slots, arrived, partial, give, take,
     spread, spread_t, serve, serve_t, docs, memory, keys, values, hidden, grad, gated, gnorm, cgrad, ngrad, stats,
-    key_grad, value_grad, grads_t, halo_out, halo_in, give_far, take_far,
+    key_grad, value_grad, grads_t, halo_in, give_far, take_far,
     load_sem, in_sem, req_send, req_recv, rep_send, rep_recv, tz_send, tz_recv, wz_send, wz_recv,
     xy_send, xy_recv, core_send, core_recv, halo_send, halo_recv, slot_send, slot_recv, ring_send, ring_recv,
     far_send, far_recv,
@@ -392,16 +402,19 @@
     for b in range(NB):
         src = wk_ref if b < NB // 2 else wv_ref
         loads.append(pltpu.make_async_copy(src.at[:, pl.ds(lanes(b).start, CB)], weights.at[b, here.z, here.core], load_sem.at[b]))
-    inputs = [pltpu.make_async_copy(hidden_ref, hidden, in_sem.at[0]), pltpu.make_async_copy(grad_ref, grad, in_sem.at[1])]
+    inputs = [pltpu.make_async_copy(hidden_ref, hidden, in_sem.at[0]), pltpu.make_async_copy(grad_ref, grad.at[pl.ds(0, TOK)], in_sem.at[1])]
     for load in loads + inputs:
         load.start()
     for c in range(NC):
-        tab[c, here.z, 0:R_DEV, :] = table_ref[:, c * CW : (c + 1) * CW].astype(BF16)
-        tab[c, here.z, R_DEV:TROWS, :] = jnp.zeros((TROWS - R_DEV, CW), BF16)
+        tab[here.z, c, 0:R_DEV, :] = table_ref[:, c * CW : (c + 1) * CW].astype(BF16)
+        tab[here.z, c, R_DEV:TROWS, :] = jnp.zeros((TROWS - R_DEV, CW), BF16)
     plan_slots(owner_ref, local_ref, expand_ref, spread, spread_t, req_out)
     greeted()
 
-    tables = [Ring(here, lambda zz, c=c: tab.at[c, zz], tz_send.at[c], tz_recv.at[c], c % 2) for c in range(NC)]
+    spans = (pl.ds(0, NC // 2 + 1), pl.ds(NC // 2 + 1, NC // 2))
+    tables = [
+        Ring(here, lambda zz, span=span: tab.at[zz, span], tz_send.at[i], tz_recv.at[i], i) for i, span in enumerate(spans)
+    ]
     blocks = [here.x, NB // 2 + here.y, NB // 2 - 1, NB - 1]
     pieces = [
         Ring(here, lambda zz, b=b: weights.at[b, zz, here.core], wz_send.at[i], wz_recv.at[i], i % 2)
@@ -412,44 +425,52 @@
         Cross(here, "y", weights, NB // 2, xy_send.at[1], xy_recv.at[1]),
     ]
     zeds = [here.zed(step) for step in (0, -1, 1, -2, 2, -3, 3, 4)]
-    for load in loads:
-        load.wait()
+    key_ring, value_ring, last_key, last_value = pieces
+    x_cross, y_cross = crosses
     for ring in tables:
-        ring.start(1)
-    for ring in pieces[:2]:
         ring.start(1)
     send_mates(here, req_out, req_in, req_send, req_recv)
     req_in[here.plane] = req_out[here.plane]
+    for load in loads + inputs:
+        load.wait()
+    early = remote(
+        grad.at[pl.ds(0, PAD)], grad.at[pl.ds(TOK, PAD)], halo_send.at[2], halo_recv.at[2], here.neighbour(-1)
+    )
+    early.start()
     plan_docs(here, lengths_ref, docs)
+    for ring in tables:
+        ring.sent(1)
+    key_ring.start(1)
+    mates_arrived(here, req_in, req_recv)
+    plan_serve(req_in, serve, serve_t)
+    key_ring.sent(1)
+    value_ring.start(1)
     for step in (1, 2, 3):
         for ring in tables:
             ring.arrived(step)
             ring.start(step + 1)
-        for ring in pieces[:2]:
+        for ring, cross in ((key_ring, x_cross), (value_ring, y_cross)):
             ring.arrived(step)
             ring.start(step + 1)
-        for cross in crosses:
             for i in (2 * step - 1, 2 * step):
                 cross.start(zeds[i], i)
-        if step == 1:
-            mates_arrived(here, req_in, req_recv)
-            plan_serve(req_in, serve, serve_t)
         if step > 1:
             for cross in crosses:
                 for i in (2 * step - 3, 2 * step - 2):
                     cross.relay(zeds[i], i)
-    for ring in pieces[2:]:
-        ring.start(1)
-    for ring in pieces[:2]:
+    last_key.start(1)
+    for ring in tables:
         ring.arrived(4)
-    for cross in crosses:
-        cross.start(zeds[Z - 1], Z - 1)
     for c in range(NC):
-        tables[c].arrived(4)
-        rows = nn(serve[...], tab[c].reshape(Z * TROWS, CW))
+        rows = nn(serve[...], tab[:, c].reshape(Z * TROWS, CW))
         reply[c] = rows.astype(BF16).reshape(PLANE, MSG, CW)
         fetched[c, here.plane] = reply[c, here.plane]
         send_mates(here, reply.at[c], fetched.at[c], rep_send.at[c], rep_recv.at[c])
+    last_key.sent(1)
+    last_value.start(1)
+    for ring, cross in ((key_ring, x_cross), (value_ring, y_cross)):
+        ring.arrived(4)
+        cross.start(zeds[Z - 1], Z - 1)
 
     def to_partner(b):
         ref = weights.at[b, :, here.core]
@@ -471,18 +492,14 @@
 
     for b in (here.x, NB // 2 + here.y):
         to_partner(b).start()
-    for ring in pieces[2:]:
-        ring.arrived(1)
-        ring.start(2)
-    for cross in crosses:
-        for i in (Z - 3, Z - 2):
-            cross.relay(zeds[i], i)
-    for step in (2, 3):
+    for step in (1, 2, 3):
         for ring in pieces[2:]:
             ring.arrived(step)
             ring.start(step + 1)
-    for load in inputs:
-        load.wait()
+        if step == 1:
+            for cross in crosses:
+                for i in (Z - 3, Z - 2):
+                    cross.relay(zeds[i], i)
     for cross in crosses:
         cross.relay(zeds[Z - 1], Z - 1)
     for step in (-1, 1):
@@ -508,52 +525,48 @@
     project_key(NB // 2 - 1)
     project_value(NB // 2 - 1)
 
+    last = TOK // TILE - 1
+
     def halo(way):
-        sign = 1 if way == 0 else -1
-        device = (here.row, lax.rem(here.col + sign + X * Y, X * Y))
-        return remote(halo_out.at[way], halo_in.at[way], halo_send.at[way], halo_recv.at[way], device)
-
-    last = TOK // TILE - 1
+        src = gated.at[pl.ds(last * TILE if way == 0 else 0, TILE)]
+        return remote(src, halo_in.at[way], halo_send.at[way], halo_recv.at[way], here.neighbour(1 - 2 * way))
 
     def gate_step(t, carry):
         gate_tile(t, keys, values, hidden, gated, gnorm, stats)
         return carry
 
-    gate_tile(last, keys, values, hidden, gated, gnorm, stats)
-    halo_out[0] = gated[TOK - TILE : TOK, :]
-    halo(0).start()
-    lax.fori_loop(0, last, gate_step, 0)
-    halo(0).wait_recv()
-    total = jnp.zeros((TILE, CB), F32)
-    for b in BLOCKS:
-        rows = halo_in[0, :, lanes(b)].astype(F32)
-        total = total + rows * rows
-    scale = mean_scale(jnp.sum(total, axis=1, keepdims=True))
-    for b in BLOCKS:
-        gnorm[0:PAD, lanes(b)] = halo_in[0, :, lanes(b)].astype(F32) * scale
-
     def conv_step(t, carry):
         conv_tile(t, docs, taps_ref, gnorm, gated, grad, cgrad, out)
         return carry
 
-    conv_tile(0, docs, taps_ref, gnorm, gated, grad, cgrad, out)
-    halo_out[1] = cgrad[0:TILE, :].astype(BF16)
-    halo(1).start()
-    lax.fori_loop(1, last + 1, conv_step, 0)
-
     def grad_step(t, carry):
         grad_tile(t, docs, taps_ref, gnorm, cgrad, grad, keys, values, hidden, stats, ngrad, key_grad, value_grad)
         return carry
 
-    lax.fori_loop(0, last, grad_step, 0)
-    halo(1).wait_recv()
-    cgrad[TOK : TOK + PAD, :] = halo_in[1].astype(F32)
-    grad_step(last, 0)
+    gate_step(last, 0)
+    halo(0).start()
+    gate_step(0, 0)
+    halo(1).start()
+    lax.fori_loop(1, last, gate_step, 0)
+    lax.fori_loop(1, last + 1, conv_step, 0)
+    for way, start in ((0, 0), (1, PAD + TOK)):
+        halo(way).wait_recv()
+        total = jnp.zeros((TILE, CB), F32)
+        for b in BLOCKS:
+            rows = halo_in[way, :, lanes(b)].astype(F32)
+            total = total + rows * rows
+        scale = mean_scale(jnp.sum(total, axis=1, keepdims=True))
+        for b in BLOCKS:
+            gnorm[start : start + PAD, lanes(b)] = halo_in[way, :, lanes(b)].astype(F32) * scale
+    early.wait_recv()
+    conv_step(0, 0)
+    conv_tile(last + 1, docs, taps_ref, gnorm, gated, grad, cgrad)
+    lax.fori_loop(0, last + 1, grad_step, 0)
 
     for b in range(NB):
         source = key_grad if b < NB // 2 else value_grad
         grads_t[b] = source[:, lanes(b)].T
-    for c in range(NC):
+    def send_slots(c):
         first, stop = c * CW // (2 * WROWS), -(-(c + 1) * CW // (2 * WROWS))
         skip = c * CW - first * 2 * WROWS
         total = jnp.zeros((CW, TOK), F32)
@@ -562,6 +575,8 @@
             total = total + nn(part, grads_t[b])
         slots[c] = nt(spread_t[...], total.astype(BF16)).astype(BF16).reshape(PLANE, MSG, CW)
         arrived[c, here.plane] = slots[c, here.plane]
+        if c >= AHEAD:
+            mates_sent(here, slots.at[c - AHEAD], slot_send.at[c - AHEAD])
         send_mates(here, slots.at[c], arrived.at[c], slot_send.at[c], slot_recv.at[c])
 
     def hop(c, way, step):
@@ -612,7 +627,11 @@
                 total = total + take_far[c - RINGS, step].astype(F32)
         row_grad[:, c * CW : (c + 1) * CW] = total[:R_DEV]
 
+    for c in range(AHEAD):
+        send_slots(c)
     for c in range(NC):
+        if c + AHEAD < NC:
+            send_slots(c + AHEAD)
         mates_arrived(here, arrived.at[c], slot_recv.at[c])
         partial[c] = nn(serve_t[...], arrived[c].reshape(PLACES, CW)).reshape(Z, TROWS, CW)
         if c < RINGS:
@@ -629,6 +648,8 @@
     for c in range(NC):
         finish(c)
 
+    value_ring.sent(1)
+    last_value.sent(1)
     for b in range(NB):
         to_partner(b).wait_send()
     for ring in tables + pieces:
@@ -636,12 +657,14 @@
     for i in range(1, Z):
         for cross in crosses:
             cross.drain(zeds[i], i)
+    early.wait_send()
     for way in range(2):
         halo(way).wait_send()
     mates_sent(here, req_out, req_send)
     for c in range(NC):
         mates_sent(here, reply.at[c], rep_send.at[c])
-        mates_sent(here, slots.at[c], slot_send.at[c])
+        if c >= NC - AHEAD:
+            mates_sent(here, slots.at[c], slot_send.at[c])
         if c < RINGS:
             for way in range(2):
                 for step in range(1, length(c, way) + 1):
@@ -668,7 +691,7 @@
         out_specs=(vmem, vmem),
         scratch_shapes=[
             pltpu.VMEM((NB, Z, 2, WROWS, CB), BF16),
-            pltpu.VMEM((NC, Z, TROWS, CW), BF16),
+            pltpu.VMEM((Z, NC, TROWS, CW), BF16),
             pltpu.VMEM((PLANE, 1, 128), F32),
             pltpu.VMEM((PLANE, 1, 128), F32),
             pltpu.VMEM(rows, BF16),
@@ -682,14 +705,14 @@
             pltpu.VMEM((PLACES, TOK), BF16),
             pltpu.VMEM((PLACES, Z * TROWS), BF16),
             pltpu.VMEM((Z * TROWS, PLACES), BF16),
-            pltpu.VMEM((TOK + 2 * PAD, 128), F32),
+            pltpu.VMEM((TOK + 3 * PAD, 128), F32),
             pltpu.VMEM((TOK, E), BF16),
             pltpu.VMEM((NB // 2, TOK, CB), F32),
             pltpu.VMEM((NB // 2, TOK, CB), F32),
             pltpu.VMEM((TOK, D), BF16),
+            pltpu.VMEM((TOK + PAD, D), BF16),
             pltpu.VMEM((TOK, D), BF16),
-            pltpu.VMEM((TOK, D), BF16),
-            pltpu.VMEM((PAD + TOK, D), F32),
+            pltpu.VMEM((PAD + TOK + PAD, D), F32),
             pltpu.VMEM((TOK + PAD, D), F32),
             pltpu.VMEM((TILE, D), F32),
             pltpu.VMEM((len(STATS), TOK, 128), F32),
@@ -697,13 +720,12 @@
             pltpu.VMEM((TOK, D), BF16),
             pltpu.VMEM((NB, CB, TOK), BF16),
             pltpu.VMEM((2, TILE, D), BF16),
-            pltpu.VMEM((2, TILE, D), BF16),
             pltpu.VMEM(fars + (TROWS, CW), BF16),
             pltpu.VMEM(fars + (TROWS, CW), BF16),
             dma((NB,)), dma((2,)), dma, dma, dma((NC,)), dma((NC,)),
-            dma((NC, 2, Z // 2)), dma((NC, 2, Z // 2)), dma((4, 2, Z // 2)), dma((4, 2, Z // 2)),
+            dma((2, 2, Z // 2)), dma((2, 2, Z // 2)), dma((4, 2, Z // 2)), dma((4, 2, Z // 2)),
             dma((2, 4, Z)), dma((2, 4, Z)), dma((NB,)), dma((NB,)),
-            dma((2,)), dma((2,)), dma((NC,)), dma((NC,)), dma(hops), dma(hops), dma(fars), dma(fars),
+            dma((3,)), dma((3,)), dma((NC,)), dma((NC,)), dma(hops), dma(hops), dma(fars), dma(fars),
         ],
         compiler_params=pltpu.CompilerParams(
             collective_id=0, has_side_effects=True, vmem_limit_bytes=56 * 1024 * 1024

time: 112 us -> 111 us (level)
  Pallas kernels: 108 us -> 106 us
    pallas_call x1, Pallas kernels: 108 us -> 106 us  [on_device(): pl.pallas_call(kernel, out_shape=(jax.ShapeDtypeStruct((TOK, D), BF16), j...]
where the time goes in v4:
time: 111 us; the launch traced here: 110 us
  Pallas kernels  106 us (95%)
  other arithmetic  1.91 us (2%)
    pallas_call x1, Pallas kernels, on_device(): pl.pallas_call(kernel, out_shape=(jax.ShapeDtypeStruct((TOK, D), BF16), j...  106 us

profile of v4, /device:TPU:1, one launch (start us, length us, event | category | flops | bytes accessed | tf_op | source)
XLA Modules:
  0.0 109.7 jit_solution(3321023646718021501)
XLA Ops:
  0.6 0.0 copy-start
  0.6 0.0 copy-start.2
  0.7 0.0 copy-start.3
  0.7 106.2 %memory_branch.1 = (bf16[128,2560]{1,0:T(8,128)(2,1)}, f32[40,1280]{1,0:T(8,128)}) custom-call(s32[1,144]{1,0:T(1,128)} %bitcast.10, s32[1,144]{1,0:T(1,128)} %local_ref.1, s32[2,128]{1,0:T(2,128)} %bitcast.11, s32[1,8]{1,0:T(1,128)} %lengths_ref.1, f32[4,2560]{1,0:T(4,128)} %taps_ref.1, f32[40,1280]{1,0:T(8,128)} %table_ref.1, bf16[128,2560]{1,0:T(8,128)(2,1)} %bitcast.8, ...), custom_call_target="tpu_custom_call" | custom-call | tf_op jit(solution)/shard_map/memory_branch/pallas_call | solution.py:687
  106.9 0.0 copy-done
  106.9 0.0 copy-done.2
  106.9 0.0 copy-done.3
  106.9 0.0 copy-start.1
  106.9 1.9 %multiply_subtract_fusion = (f32[40,1280]{1,0:T(8,128)}, f32[40,1280]{1,0:T(8,128)}, f32[40,1280]{1,0:T(8,128)}) fusion(f32[40,1280]{1,0:T(8,128)S(1)} %copy-done, f32[40,1280]{1,0:T(8,128)} %get-tuple-element.7, f32[40,1280]{1,0:T(8,128)S(1)} %copy-done.2, f32[40,1280]{1,0:T(8,128)S(1)} %copy-done.3), kind=kLoop, calls=%fused_computation.2 | loop fusion | flops 768000 | bytes 1433600 | tf_op jit(solution)/shard_map/sub | solution.py:385
  108.9 0.0 copy-done.1
  108.9 0.8 copy.17
Async XLA Ops:
  0.6 106.3 %copy-start = (f32[40,1280]{1,0:T(8,128)S(1)}, f32[40,1280]{1,0:T(8,128)}, u32[]{:S(2)}) copy-start(f32[40,1280]{1,0:T(8,128)} %table_ref.1) | copy-start | bytes 614404
  0.6 106.3 %copy-start.2 = (f32[40,1280]{1,0:T(8,128)S(1)}, f32[40,1280]{1,0:T(8,128)}, u32[]{:S(2)}) copy-start(f32[40,1280]{1,0:T(8,128)} %param.18) | copy-start | bytes 614404
  0.7 106.3 %copy-start.3 = (f32[40,1280]{1,0:T(8,128)S(1)}, f32[40,1280]{1,0:T(8,128)}, u32[]{:S(2)}) copy-start(f32[40,1280]{1,0:T(8,128)} %param.19) | copy-start | bytes 614404
  106.9 1.9 %copy-start.1 = (bf16[128,2560]{1,0:T(8,128)(2,1)S(1)}, bf16[128,2560]{1,0:T(8,128)(2,1)}, u32[]{:S(2)}) copy-start(bf16[128,2560]{1,0:T(8,128)(2,1)} %get-tuple-element.6) | copy-start | bytes 1966084

commit v5 on v4

--- a/solution.py
+++ b/solution.py
@@ -20,7 +20,7 @@
 TOK, U, R_DEV = 128, 144, 40
 CW = 256
 NC = E // CW
-RINGS = 3
+RINGS = 2
 AHEAD = 2
 TROWS = 48
 MSG = 2 * Z
@@ -253,6 +253,9 @@
                 self.base + self.place(-2 * sign), zz, self.here.core, :, pl.ds((way - 2) * (CB // 2), CB // 2)
             ]
         return remote(ref, ref, self.send.at[way, i], self.recv.at[way, i], self.at(-sign))
+
+    def block(self, step):
+        return self.base + self.place(step)
 
     def start(self, zz, i):
         for way in (0, 1):
@@ -393,7 +396,7 @@
     spread, spread_t, serve, serve_t, docs, memory, keys, values, hidden, grad, gated, gnorm, cgrad, ngrad, stats,
     key_grad, value_grad, grads_t, halo_in, give_far, take_far,
     load_sem, in_sem, req_send, req_recv, rep_send, rep_recv, tz_send, tz_recv, wz_send, wz_recv,
-    xy_send, xy_recv, core_send, core_recv, halo_send, halo_recv, slot_send, slot_recv, ring_send, ring_recv,
+    xy_send, xy_recv, core_send, core_recv, own_send, own_recv, halo_send, halo_recv, slot_send, slot_recv, ring_send, ring_recv,
     far_send, far_recv,
 ):
     here = Here()
@@ -425,6 +428,19 @@
         Cross(here, "y", weights, NB // 2, xy_send.at[1], xy_recv.at[1]),
     ]
     zeds = [here.zed(step) for step in (0, -1, 1, -2, 2, -3, 3, 4)]
+    def to_partner(b, zz):
+        ref = weights.at[b, zz, here.core]
+        return remote(ref, ref, core_send.at[b, zz], core_recv.at[b, zz], here.partner())
+
+    def own_to_partner():
+        ref = weights.at[:, here.z, here.core]
+        return remote(ref, ref, own_send, own_recv, here.partner())
+
+    def from_partner(b):
+        for i in range(1, Z):
+            ref = weights.at[b, zeds[i], 1 - here.core]
+            remote(ref, ref, core_send.at[b, zeds[i]], core_recv.at[b, zeds[i]], here.partner()).wait_recv()
+
     key_ring, value_ring, last_key, last_value = pieces
     x_cross, y_cross = crosses
     for ring in tables:
@@ -437,6 +453,7 @@
         grad.at[pl.ds(0, PAD)], grad.at[pl.ds(TOK, PAD)], halo_send.at[2], halo_recv.at[2], here.neighbour(-1)
     )
     early.start()
+    own_to_partner().start()
     plan_docs(here, lengths_ref, docs)
     for ring in tables:
         ring.sent(1)
@@ -454,10 +471,13 @@
             ring.start(step + 1)
             for i in (2 * step - 1, 2 * step):
                 cross.start(zeds[i], i)
+                to_partner(cross.block(0), zeds[i]).start()
         if step > 1:
             for cross in crosses:
                 for i in (2 * step - 3, 2 * step - 2):
                     cross.relay(zeds[i], i)
+                    for side in (-1, 1):
+                        to_partner(cross.block(side), zeds[i]).start()
     last_key.start(1)
     for ring in tables:
         ring.arrived(4)
@@ -471,14 +491,7 @@
     for ring, cross in ((key_ring, x_cross), (value_ring, y_cross)):
         ring.arrived(4)
         cross.start(zeds[Z - 1], Z - 1)
-
-    def to_partner(b):
-        ref = weights.at[b, :, here.core]
-        return remote(ref, ref, core_send.at[b], core_recv.at[b], here.partner())
-
-    def from_partner(b):
-        ref = weights.at[b, :, 1 - here.core]
-        remote(ref, ref, core_send.at[b], core_recv.at[b], here.partner()).wait_recv()
+        to_partner(cross.block(0), zeds[Z - 1]).start()
 
     def project(b):
         from_partner(b)
@@ -490,35 +503,40 @@
     def project_value(b):
         values[b] = project(NB // 2 + b)
 
-    for b in (here.x, NB // 2 + here.y):
-        to_partner(b).start()
     for step in (1, 2, 3):
-        for ring in pieces[2:]:
+        for ring, b in zip(pieces[2:], (NB // 2 - 1, NB - 1)):
             ring.arrived(step)
             ring.start(step + 1)
+            for i in (2 * step - 1, 2 * step):
+                to_partner(b, zeds[i]).start()
         if step == 1:
             for cross in crosses:
                 for i in (Z - 3, Z - 2):
                     cross.relay(zeds[i], i)
+                    for side in (-1, 1):
+                        to_partner(cross.block(side), zeds[i]).start()
+        else:
+            for cross in crosses:
+                for i in (2 * step - 3, 2 * step - 2):
+                    cross.finish(zeds[i], i)
+                    to_partner(cross.block(2), zeds[i]).start()
     for cross in crosses:
         cross.relay(zeds[Z - 1], Z - 1)
-    for step in (-1, 1):
-        to_partner(here.exx(step)).start()
-        to_partner(NB // 2 + here.wye(step)).start()
+        for side in (-1, 1):
+            to_partner(cross.block(side), zeds[Z - 1]).start()
     for c in range(NC):
         mates_arrived(here, fetched.at[c], rep_recv.at[c])
         memory[:, c * CW : (c + 1) * CW] = nn(spread[...], fetched[c].reshape(PLACES, CW)).astype(BF16)
+    own_to_partner().wait_recv()
     project_key(here.x)
     project_value(here.y)
-    for i in range(1, Z):
+    for ring, b in zip(pieces[2:], (NB // 2 - 1, NB - 1)):
+        ring.arrived(4)
+        to_partner(b, zeds[Z - 1]).start()
+    for i in range(5, Z):
         for cross in crosses:
             cross.finish(zeds[i], i)
-    to_partner(here.exx(2)).start()
-    to_partner(NB // 2 + here.wye(2)).start()
-    for ring in pieces[2:]:
-        ring.arrived(4)
-    to_partner(NB // 2 - 1).start()
-    to_partner(NB - 1).start()
+            to_partner(cross.block(2), zeds[i]).start()
     for step in (-1, 1, 2):
         project_key(here.exx(step))
         project_value(here.wye(step))
@@ -650,8 +668,10 @@
 
     value_ring.sent(1)
     last_value.sent(1)
+    own_to_partner().wait_send()
     for b in range(NB):
-        to_partner(b).wait_send()
+        for i in range(1, Z):
+            to_partner(b, zeds[i]).wait_send()
     for ring in tables + pieces:
         ring.drain()
     for i in range(1, Z):
@@ -724,7 +744,7 @@
             pltpu.VMEM(fars + (TROWS, CW), BF16),
             dma((NB,)), dma((2,)), dma, dma, dma((NC,)), dma((NC,)),
             dma((2, 2, Z // 2)), dma((2, 2, Z // 2)), dma((4, 2, Z // 2)), dma((4, 2, Z // 2)),
-            dma((2, 4, Z)), dma((2, 4, Z)), dma((NB,)), dma((NB,)),
+            dma((2, 4, Z)), dma((2, 4, Z)), dma((NB, Z)), dma((NB, Z)), dma, dma,
             dma((3,)), dma((3,)), dma((NC,)), dma((NC,)), dma(hops), dma(hops), dma(fars), dma(fars),
         ],
         compiler_params=pltpu.CompilerParams(

time: 111 us -> 111 us (level)
  no operation moved by 1% of the time
where the time goes in v5:
time: 111 us; the launch traced here: 110 us
  Pallas kernels  107 us (96%)
  other arithmetic  1.91 us (2%)
    pallas_call x1, Pallas kernels, on_device(): pl.pallas_call(kernel, out_shape=(jax.ShapeDtypeStruct((TOK, D), BF16), j...  107 us

profile of v5, /device:TPU:1, one launch (start us, length us, event | category | flops | bytes accessed | tf_op | source)
XLA Modules:
  0.0 110.5 jit_solution(1682498900102778267)
XLA Ops:
  0.6 0.0 copy-start
  0.6 0.0 copy-start.2
  0.7 0.0 copy-start.3
  0.7 107.0 %memory_branch.1 = (bf16[128,2560]{1,0:T(8,128)(2,1)}, f32[40,1280]{1,0:T(8,128)}) custom-call(s32[1,144]{1,0:T(1,128)} %bitcast.10, s32[1,144]{1,0:T(1,128)} %local_ref.1, s32[2,128]{1,0:T(2,128)} %bitcast.11, s32[1,8]{1,0:T(1,128)} %lengths_ref.1, f32[4,2560]{1,0:T(4,128)} %taps_ref.1, f32[40,1280]{1,0:T(8,128)} %table_ref.1, bf16[128,2560]{1,0:T(8,128)(2,1)} %bitcast.8, ...), custom_call_target="tpu_custom_call" | custom-call | tf_op jit(solution)/shard_map/memory_branch/pallas_call | solution.py:707
  107.7 0.0 copy-done
  107.7 0.0 copy-done.2
  107.7 0.0 copy-done.3
  107.7 0.0 copy-start.1
  107.8 1.9 %multiply_subtract_fusion = (f32[40,1280]{1,0:T(8,128)}, f32[40,1280]{1,0:T(8,128)}, f32[40,1280]{1,0:T(8,128)}) fusion(f32[40,1280]{1,0:T(8,128)S(1)} %copy-done, f32[40,1280]{1,0:T(8,128)} %get-tuple-element.7, f32[40,1280]{1,0:T(8,128)S(1)} %copy-done.2, f32[40,1280]{1,0:T(8,128)S(1)} %copy-done.3), kind=kLoop, calls=%fused_computation.2 | loop fusion | flops 768000 | bytes 1433600 | tf_op jit(solution)/shard_map/sub | solution.py:388
  109.7 0.0 copy-done.1
  109.7 0.8 copy.17
Async XLA Ops:
  0.6 107.1 %copy-start = (f32[40,1280]{1,0:T(8,128)S(1)}, f32[40,1280]{1,0:T(8,128)}, u32[]{:S(2)}) copy-start(f32[40,1280]{1,0:T(8,128)} %table_ref.1) | copy-start | bytes 614404
  0.6 107.1 %copy-start.2 = (f32[40,1280]{1,0:T(8,128)S(1)}, f32[40,1280]{1,0:T(8,128)}, u32[]{:S(2)}) copy-start(f32[40,1280]{1,0:T(8,128)} %param.18) | copy-start | bytes 614404
  0.7 107.1 %copy-start.3 = (f32[40,1280]{1,0:T(8,128)S(1)}, f32[40,1280]{1,0:T(8,128)}, u32[]{:S(2)}) copy-start(f32[40,1280]{1,0:T(8,128)} %param.19) | copy-start | bytes 614404
  107.7 1.9 %copy-start.1 = (bf16[128,2560]{1,0:T(8,128)(2,1)S(1)}, bf16[128,2560]{1,0:T(8,128)(2,1)}, u32[]{:S(2)}) copy-start(bf16[128,2560]{1,0:T(8,128)(2,1)} %get-tuple-element.6) | copy-start | bytes 1966084

commit v6 on v5

--- a/solution.py
+++ b/solution.py
@@ -219,14 +219,9 @@
                 got.append(-sign * step)
         return got
 
-    def sent(self, step):
-        for way in range(2):
-            if step <= self.steps(way):
-                self.copy(way, step).wait_send()
-
     def drain(self):
         for way in range(2):
-            for step in range(2, self.steps(way) + 1):
+            for step in range(1, self.steps(way) + 1):
                 self.copy(way, step).wait_send()
 
 
@@ -412,6 +407,7 @@
         tab[here.z, c, 0:R_DEV, :] = table_ref[:, c * CW : (c + 1) * CW].astype(BF16)
         tab[here.z, c, R_DEV:TROWS, :] = jnp.zeros((TROWS - R_DEV, CW), BF16)
     plan_slots(owner_ref, local_ref, expand_ref, spread, spread_t, req_out)
+    plan_docs(here, lengths_ref, docs)
     greeted()
 
     spans = (pl.ds(0, NC // 2 + 1), pl.ds(NC // 2 + 1, NC // 2))
@@ -441,44 +437,41 @@
             ref = weights.at[b, zeds[i], 1 - here.core]
             remote(ref, ref, core_send.at[b, zeds[i]], core_recv.at[b, zeds[i]], here.partner()).wait_recv()
 
-    key_ring, value_ring, last_key, last_value = pieces
+    key_ring, value_ring = pieces[:2]
     x_cross, y_cross = crosses
+    for load in loads + inputs:
+        load.wait()
+    for ring in pieces[:2]:
+        ring.start(1)
     for ring in tables:
         ring.start(1)
     send_mates(here, req_out, req_in, req_send, req_recv)
     req_in[here.plane] = req_out[here.plane]
-    for load in loads + inputs:
-        load.wait()
     early = remote(
         grad.at[pl.ds(0, PAD)], grad.at[pl.ds(TOK, PAD)], halo_send.at[2], halo_recv.at[2], here.neighbour(-1)
     )
     early.start()
     own_to_partner().start()
-    plan_docs(here, lengths_ref, docs)
-    for ring in tables:
-        ring.sent(1)
-    key_ring.start(1)
     mates_arrived(here, req_in, req_recv)
     plan_serve(req_in, serve, serve_t)
-    key_ring.sent(1)
-    value_ring.start(1)
     for step in (1, 2, 3):
-        for ring in tables:
-            ring.arrived(step)
-            ring.start(step + 1)
         for ring, cross in ((key_ring, x_cross), (value_ring, y_cross)):
             ring.arrived(step)
             ring.start(step + 1)
             for i in (2 * step - 1, 2 * step):
                 cross.start(zeds[i], i)
                 to_partner(cross.block(0), zeds[i]).start()
+        for ring in tables:
+            ring.arrived(step)
+            ring.start(step + 1)
         if step > 1:
             for cross in crosses:
                 for i in (2 * step - 3, 2 * step - 2):
                     cross.relay(zeds[i], i)
                     for side in (-1, 1):
                         to_partner(cross.block(side), zeds[i]).start()
-    last_key.start(1)
+    for ring in pieces[2:]:
+        ring.start(1)
     for ring in tables:
         ring.arrived(4)
     for c in range(NC):
@@ -486,8 +479,6 @@
         reply[c] = rows.astype(BF16).reshape(PLANE, MSG, CW)
         fetched[c, here.plane] = reply[c, here.plane]
         send_mates(here, reply.at[c], fetched.at[c], rep_send.at[c], rep_recv.at[c])
-    last_key.sent(1)
-    last_value.start(1)
     for ring, cross in ((key_ring, x_cross), (value_ring, y_cross)):
         ring.arrived(4)
         cross.start(zeds[Z - 1], Z - 1)
@@ -666,8 +657,6 @@
     for c in range(NC):
         finish(c)
 
-    value_ring.sent(1)
-    last_value.sent(1)
     own_to_partner().wait_send()
     for b in range(NB):
         for i in range(1, Z):

time: 111 us -> 109 us (0.982)
  Pallas kernels: 107 us -> 104 us
    pallas_call x1, Pallas kernels: 107 us -> 104 us  [on_device(): pl.pallas_call(kernel, out_shape=(jax.ShapeDtypeStruct((TOK, D), BF16), j...]
where the time goes in v6:
time: 109 us; the launch traced here: 108 us
  Pallas kernels  104 us (95%)
  other arithmetic  1.91 us (2%)
    pallas_call x1, Pallas kernels, on_device(): pl.pallas_call(kernel, out_shape=(jax.ShapeDtypeStruct((TOK, D), BF16), j...  104 us

profile of v6, /device:TPU:1, one launch (start us, length us, event | category | flops | bytes accessed | tf_op | source)
XLA Modules:
  0.0 107.8 jit_solution(10195498538011223437)
XLA Ops:
  0.6 0.0 copy-start
  0.6 0.0 copy-start.2
  0.7 0.0 copy-start.3
  0.7 104.3 %memory_branch.1 = (bf16[128,2560]{1,0:T(8,128)(2,1)}, f32[40,1280]{1,0:T(8,128)}) custom-call(s32[1,144]{1,0:T(1,128)} %bitcast.10, s32[1,144]{1,0:T(1,128)} %local_ref.1, s32[2,128]{1,0:T(2,128)} %bitcast.11, s32[1,8]{1,0:T(1,128)} %lengths_ref.1, f32[4,2560]{1,0:T(4,128)} %taps_ref.1, f32[40,1280]{1,0:T(8,128)} %table_ref.1, bf16[128,2560]{1,0:T(8,128)(2,1)} %bitcast.8, ...), custom_call_target="tpu_custom_call" | custom-call | tf_op jit(solution)/shard_map/memory_branch/pallas_call | solution.py:696
  105.0 0.0 copy-done
  105.0 0.0 copy-done.2
  105.0 0.0 copy-done.3
  105.0 0.0 copy-start.1
  105.1 1.9 %multiply_subtract_fusion = (f32[40,1280]{1,0:T(8,128)}, f32[40,1280]{1,0:T(8,128)}, f32[40,1280]{1,0:T(8,128)}) fusion(f32[40,1280]{1,0:T(8,128)S(1)} %copy-done, f32[40,1280]{1,0:T(8,128)} %get-tuple-element.7, f32[40,1280]{1,0:T(8,128)S(1)} %copy-done.2, f32[40,1280]{1,0:T(8,128)S(1)} %copy-done.3), kind=kLoop, calls=%fused_computation.2 | loop fusion | flops 768000 | bytes 1433600 | tf_op jit(solution)/shard_map/sub | solution.py:383
  107.0 0.0 copy-done.1
  107.0 0.8 copy.17
Async XLA Ops:
  0.6 104.4 %copy-start = (f32[40,1280]{1,0:T(8,128)S(1)}, f32[40,1280]{1,0:T(8,128)}, u32[]{:S(2)}) copy-start(f32[40,1280]{1,0:T(8,128)} %table_ref.1) | copy-start | bytes 614404
  0.6 104.4 %copy-start.2 = (f32[40,1280]{1,0:T(8,128)S(1)}, f32[40,1280]{1,0:T(8,128)}, u32[]{:S(2)}) copy-start(f32[40,1280]{1,0:T(8,128)} %param.18) | copy-start | bytes 614404
  0.7 104.4 %copy-start.3 = (f32[40,1280]{1,0:T(8,128)S(1)}, f32[40,1280]{1,0:T(8,128)}, u32[]{:S(2)}) copy-start(f32[40,1280]{1,0:T(8,128)} %param.19) | copy-start | bytes 614404
  105.0 1.9 %copy-start.1 = (bf16[128,2560]{1,0:T(8,128)(2,1)S(1)}, bf16[128,2560]{1,0:T(8,128)(2,1)}, u32[]{:S(2)}) copy-start(bf16[128,2560]{1,0:T(8,128)(2,1)} %get-tuple-element.6) | copy-start | bytes 1966084

commit v7 on v6

--- a/solution.py
+++ b/solution.py
@@ -556,8 +556,8 @@
     halo(0).start()
     gate_step(0, 0)
     halo(1).start()
-    lax.fori_loop(1, last, gate_step, 0)
-    lax.fori_loop(1, last + 1, conv_step, 0)
+    lax.fori_loop(1, last, gate_step, 0, unroll=True)
+    lax.fori_loop(1, last + 1, conv_step, 0, unroll=True)
     for way, start in ((0, 0), (1, PAD + TOK)):
         halo(way).wait_recv()
         total = jnp.zeros((TILE, CB), F32)
@@ -570,7 +570,7 @@
     early.wait_recv()
     conv_step(0, 0)
     conv_tile(last + 1, docs, taps_ref, gnorm, gated, grad, cgrad)
-    lax.fori_loop(0, last + 1, grad_step, 0)
+    lax.fori_loop(0, last + 1, grad_step, 0, unroll=True)
 
     for b in range(NB):
         source = key_grad if b < NB // 2 else value_grad

time: 109 us -> 108 us (level)
    pallas_call x1, Pallas kernels: 104 us -> 103 us  [on_device(): pl.pallas_call(kernel, out_shape=(jax.ShapeDtypeStruct((TOK, D), BF16), j...]
where the time goes in v7:
time: 108 us; the launch traced here: 106 us
  Pallas kernels  103 us (95%)
  other arithmetic  1.91 us (2%)
    pallas_call x1, Pallas kernels, on_device(): pl.pallas_call(kernel, out_shape=(jax.ShapeDtypeStruct((TOK, D), BF16), j...  103 us

profile of v7, /device:TPU:1, one launch (start us, length us, event | category | flops | bytes accessed | tf_op | source)
XLA Modules:
  0.0 106.3 jit_solution(8476727681027179694)
XLA Ops:
  0.6 0.0 copy-start
  0.6 0.0 copy-start.2
  0.7 0.0 copy-start.3
  0.7 102.9 %memory_branch.1 = (bf16[128,2560]{1,0:T(8,128)(2,1)}, f32[40,1280]{1,0:T(8,128)}) custom-call(s32[1,144]{1,0:T(1,128)} %bitcast.10, s32[1,144]{1,0:T(1,128)} %local_ref.1, s32[2,128]{1,0:T(2,128)} %bitcast.11, s32[1,8]{1,0:T(1,128)} %lengths_ref.1, f32[4,2560]{1,0:T(4,128)} %taps_ref.1, f32[40,1280]{1,0:T(8,128)} %table_ref.1, bf16[128,2560]{1,0:T(8,128)(2,1)} %bitcast.8, ...), custom_call_target="tpu_custom_call" | custom-call | tf_op jit(solution)/shard_map/memory_branch/pallas_call | solution.py:696
  103.5 0.0 copy-done
  103.5 0.0 copy-done.2
  103.5 0.0 copy-done.3
  103.6 0.0 copy-start.1
  103.6 1.9 %multiply_subtract_fusion = (f32[40,1280]{1,0:T(8,128)}, f32[40,1280]{1,0:T(8,128)}, f32[40,1280]{1,0:T(8,128)}) fusion(f32[40,1280]{1,0:T(8,128)S(1)} %copy-done, f32[40,1280]{1,0:T(8,128)} %get-tuple-element.7, f32[40,1280]{1,0:T(8,128)S(1)} %copy-done.2, f32[40,1280]{1,0:T(8,128)S(1)} %copy-done.3), kind=kLoop, calls=%fused_computation.2 | loop fusion | flops 768000 | bytes 1433600 | tf_op jit(solution)/shard_map/sub | solution.py:383
  105.5 0.0 copy-done.1
  105.5 0.8 copy.17
Async XLA Ops:
  0.6 102.9 %copy-start = (f32[40,1280]{1,0:T(8,128)S(1)}, f32[40,1280]{1,0:T(8,128)}, u32[]{:S(2)}) copy-start(f32[40,1280]{1,0:T(8,128)} %table_ref.1) | copy-start | bytes 614404
  0.6 102.9 %copy-start.2 = (f32[40,1280]{1,0:T(8,128)S(1)}, f32[40,1280]{1,0:T(8,128)}, u32[]{:S(2)}) copy-start(f32[40,1280]{1,0:T(8,128)} %param.18) | copy-start | bytes 614404
  0.7 102.9 %copy-start.3 = (f32[40,1280]{1,0:T(8,128)S(1)}, f32[40,1280]{1,0:T(8,128)}, u32[]{:S(2)}) copy-start(f32[40,1280]{1,0:T(8,128)} %param.19) | copy-start | bytes 614404
  103.6 1.9 %copy-start.1 = (bf16[128,2560]{1,0:T(8,128)(2,1)S(1)}, bf16[128,2560]{1,0:T(8,128)(2,1)}, u32[]{:S(2)}) copy-start(bf16[128,2560]{1,0:T(8,128)(2,1)} %get-tuple-element.6) | copy-start | bytes 1966084
